TPU v7x, 256 devices: a whole 4x4x8 slice. The times are simulated.
256 devices in a mesh: lev: 4 (over z_lo, core), row: 64 (over x, y, z_hi).
Axes of the slice: x: 4, y: 4, z: 8 (z_hi: 4, z_lo: 2; z = z_hi * 2 + z_lo), core: 2. Of those that a mesh axis runs over, the one named last changes fastest.
Arguments:
- wind_east: float32 [16, 1024, 1024], P('lev', 'row'), may hold values from -3 to 3
- wind_north: float32 [16, 1024, 1024], P('lev', 'row'), may hold values from -3 to 3
- thickness: float32 [16, 1024, 1024], P('lev', 'row'), may hold values from 0.5 to 2
- tracer_one: float32 [16, 1024, 1024], P('lev', 'row'), may hold values from 0 to 1
- tracer_two: float32 [16, 1024, 1024], P('lev', 'row'), may hold values from 0.1 to 1
- theta_step: float32 [16], replicated, may hold values from 0.5 to 2
- surface_geopot: float32 [1024, 1024], P('row'), may hold values from -12 to 12
- map_factor: float32 [1024, 1024], P('row'), may hold values from 0.5 to 2
- active_layers: int32 [1024, 1024], P('row'), may hold values from 8 to 16
Outputs:
- east_out: float32 [16, 1024, 1024], P('lev', 'row')
- north_out: float32 [16, 1024, 1024], P('lev', 'row')
- thickness_out: float32 [16, 1024, 1024], P('lev', 'row')
- tracer_one_out: float32 [16, 1024, 1024], P('lev', 'row')
- tracer_two_out: float32 [16, 1024, 1024], P('lev', 'row')
Inputs may be any that keep to these rules, and one draw needn't show every extreme that they name: Layers k with k >= active_layers of their column are below ground and keep their values.
All inputs are finite; a program needn't handle non-finite values.
Results may differ from a plain program's by a relative error of at most 0.00002.
Values sent between devices are 32-bit elements; how exact they have to be, the bound alone decides.
A program may use at most 64 MiB of HBM per device.

v0:
```python
import jax
import jax.numpy as jnp
from jax import lax
from jax.sharding import PartitionSpec as P

OUTER = 2


time_step = 0.05
top_pressure = 0.1
exner_power = 2.0 / 7.0


def carried_in(part, axis, combine, identity, reverse):
    count = lax.axis_size(axis)
    place = lax.axis_index(axis)
    ahead = count - 1 - place if reverse else place
    gathered = lax.all_gather(part, axis)
    state = jnp.zeros_like(part) + jnp.asarray(identity, part.dtype)

    def one(turn, state):
        source = count - 1 - turn if reverse else turn
        return combine(state, lax.dynamic_index_in_dim(gathered, source, 0, False))

    return lax.fori_loop(0, ahead, one, state)


def extended(block, sides, width):
    for axis, dim in sides:
        count = lax.axis_size(axis)
        forward = [(i, i + 1) for i in range(count - 1)]
        forward.append((count - 1, 0))
        backward = [(target, source) for source, target in forward]
        low = lax.ppermute(
            lax.slice_in_dim(block, block.shape[dim] - width, None, axis=dim), axis, forward
        )
        high = lax.ppermute(lax.slice_in_dim(block, 0, width, axis=dim), axis, backward)
        block = jnp.concatenate([low, block, high], axis=dim)
    return block


def add_up(earlier, later):
    return earlier + later


def potential_field(mass_field, theta_own, geopot, levels):
    inside = jnp.cumsum(jnp.abs(mass_field), axis=0)
    zeros_plane = jnp.zeros(inside.shape[1:], jnp.float32)
    offset_above = carried_in(inside[-1], "lev", add_up, zeros_plane, False)
    pressure = top_pressure + (inside + offset_above[None]) / levels
    weighted = theta_own[:, None, None] * pressure**exner_power
    summed = jnp.flip(jnp.cumsum(jnp.flip(weighted, 0), axis=0), 0)
    offset_below = carried_in(summed[0], "lev", add_up, zeros_plane, True)
    return geopot[None] + (summed + offset_below[None])


def row_diff(values):
    return (values[:, 2:] - values[:, :-2]) * 0.5


def column_diff(values):
    padded = jnp.pad(values, ((0, 0), (0, 0), (1, 1)))
    return (padded[:, :, 2:] - padded[:, :, :-2]) * 0.5


def edge_diff(values):
    padded = jnp.pad(values, ((0, 0), (0, 0), (1, 1)), mode="edge")
    return (padded[:, :, 2:] - padded[:, :, :-2]) * 0.5


def tendency(padded, potential, metric, active, coriolis):
    east_wide, north_wide, mass_wide = (padded[0], padded[1], padded[2])
    east_mid = east_wide[:, 1:-1]
    north_mid = north_wide[:, 1:-1]
    metric_mid = metric[None, 1:-1]
    flux_east = mass_wide * east_wide / metric[None]
    flux_north = mass_wide[:, 1:-1] * north_mid / metric_mid
    d_mass = -(metric_mid * metric_mid) * (row_diff(flux_east) + column_diff(flux_north))

    def carried(values):
        return -metric_mid * (
            east_mid * row_diff(values) + north_mid * column_diff(values[:, 1:-1])
        )

    d_east = carried(east_wide) + coriolis * north_mid - metric_mid * row_diff(potential)
    d_north = carried(north_wide) - coriolis * east_mid - metric_mid * edge_diff(potential[:, 1:-1])
    return (
        jnp.stack([d_east, d_north, d_mass, carried(padded[3]), carried(padded[4])]) * active[None]
    )


def local(
    wind_east,
    wind_north,
    thickness,
    tracer_one,
    tracer_two,
    theta_step,
    surface_geopot,
    map_factor,
    active_layers,
):
    layers = thickness.shape[0]
    columns = thickness.shape[2]
    levels = layers * lax.axis_size("lev")
    first_layer = lax.axis_index("lev") * layers
    theta_own = lax.dynamic_slice_in_dim(theta_step, first_layer, layers)
    layer_index = first_layer + lax.broadcasted_iota(jnp.int32, (layers, 1, 1), 0)
    coriolis = 0.5 + lax.broadcasted_iota(jnp.float32, (1, columns), 1) / columns
    fields = jnp.stack([wind_east, wind_north, thickness, tracer_one, tracer_two])
    section_fractions = (1.0 / 3.0, 0.5, 1.0)
    active = (layer_index < active_layers[None]).astype(jnp.float32)
    metric = extended(map_factor, (("row", 0),), 1)
    for outer_step in range(OUTER):
        potential = potential_field(fields[2], theta_own, surface_geopot, levels)
        potential = extended(potential, (("row", 1),), 1)
        current = fields
        for fraction in section_fractions:
            padded = extended(current, (("row", 2),), 1)
            current = fields + time_step * fraction * tendency(
                padded, potential, metric, active, coriolis
            )
        fields = current
    return (fields[0], fields[1], fields[2], fields[3], fields[4])


def solution(mesh):
    placed = (
        P("lev", "row", None),
        P("lev", "row", None),
        P("lev", "row", None),
        P("lev", "row", None),
        P("lev", "row", None),
        P(),
        P("row", None),
        P("row", None),
        P("row", None),
    )
    return jax.shard_map(
        local,
        mesh=mesh,
        in_specs=placed,
        out_specs=(
            P("lev", "row", None),
            P("lev", "row", None),
            P("lev", "row", None),
            P("lev", "row", None),
            P("lev", "row", None),
        ),
        check_vma=False,
    )
```

profile of v0, /device:TPU:1, one launch (start us, length us, event | category | flops | bytes accessed | tf_op | source)
XLA Modules:
  0.0 140.9 jit_solution(17213439170428396001)
XLA Ops:
  0.6 0.8 fusion.299
  1.4 3.8 %collective-permute-start.4 = (f32[1,1024]{1,0:T(1,128)S(1)}, f32[1,1024]{1,0:T(1,128)S(1)}, u32[]{:S(2)}, u32[]{:S(2)}) collective-permute-start(f32[1,1024]{1,0:T(1,128)S(1)} %get-tuple-element.269), channel_id=1, source_target_pairs={{0,1},{1,2},{2,3},{3,4},{4,5},{5,6},{6,7},{7,8},{8,9},{9,10},{10,1... | collective-permute-start | bytes 12296 | tf_op jit(solution)/shard_map/ppermute | solution.py:34
  5.2 7.8 %collective-permute-start.5 = (f32[1,1024]{1,0:T(1,128)S(1)}, f32[1,1024]{1,0:T(1,128)S(1)}, u32[]{:S(2)}, u32[]{:S(2)}) collective-permute-start(f32[1,1024]{1,0:T(1,128)S(1)} %get-tuple-element.270), channel_id=1, source_target_pairs={{1,0},{2,1},{3,2},{4,3},{5,4},{6,5},{7,6},{8,7},{9,8},{10,9},{11,1... | collective-permute-start | bytes 12296 | tf_op jit(solution)/shard_map/ppermute | solution.py:37
  13.0 1.0 fusion.287
  14.0 6.6 %all_gather.12 = f32[4,16,1024]{2,1,0:T(8,128)S(1)} all-gather(f32[1,16,1024]{2,1,0:T(8,128)S(1)} %slice.936), channel_id=1, replica_groups=mesh['lev'=4,'row'=64] {'lev'}, dimensions={0}, use_global_device_ids=true | all-gather | bytes 327680 | tf_op jit(solution)/shard_map/all_gather | solution.py:18
  20.9 1.0 fusion.300
  21.9 6.0 %all_gather.13 = f32[4,16,1024]{2,1,0:T(8,128)S(1)} all-gather(f32[1,16,1024]{2,1,0:T(8,128)S(1)} %slice.937), channel_id=1, replica_groups=mesh['lev'=4,'row'=64] {'lev'}, dimensions={0}, use_global_device_ids=true | all-gather | bytes 327680 | tf_op jit(solution)/shard_map/all_gather | solution.py:18
  28.1 2.6 %collective-permute-start.2 = (f32[4,1,1024]{2,1,0:T(1,128)S(1)}, f32[4,1,1024]{2,1,0:T(1,128)S(1)}, u32[]{:S(2)}, u32[]{:S(2)}) collective-permute-start(f32[4,1,1024]{2,1,0:T(1,128)S(1)} %get-tuple-element.264), channel_id=1, source_target_pairs={{1,0},{2,1},{3,2},{4,3},{5,4},{6,5},{7,6},{8,7},{9,8},{10,9},{11,1... | collective-permute-start | bytes 49160 | tf_op jit(solution)/shard_map/ppermute | solution.py:37
  31.2 0.4 copy-done.1
  31.9 7.9 %collective-permute-start.1 = (f32[5,4,1,1024]{3,2,1,0:T(1,128)S(1)}, f32[5,4,1,1024]{3,2,1,0:T(1,128)S(1)}, u32[]{:S(2)}, u32[]{:S(2)}) collective-permute-start(f32[5,4,1,1024]{3,2,1,0:T(1,128)S(1)} %get-tuple-element.245), channel_id=1, source_target_pairs={{1,0},{2,1},{3,2},{4,3},{5,4},{6,5},{7,6},{8,7},{9,8},{10,9},{11,1... | collective-permute-start | bytes 245768 | tf_op jit(solution)/shard_map/ppermute | solution.py:37
  39.8 1.5 %collective-permute-done = f32[5,4,1,1024]{3,2,1,0:T(1,128)S(1)} collective-permute-done((f32[5,4,1,1024]{3,2,1,0:T(1,128)S(1)}, f32[5,4,1,1024]{3,2,1,0:T(1,128)S(1)}, u32[]{:S(2)}, u32[]{:S(2)}) %collective-permute-start) | collective-permute-done | bytes 81952 | tf_op jit(solution)/shard_map/ppermute | solution.py:34
  41.3 1.7 %collective-permute-done.1 = f32[5,4,1,1024]{3,2,1,0:T(1,128)S(1)} collective-permute-done((f32[5,4,1,1024]{3,2,1,0:T(1,128)S(1)}, f32[5,4,1,1024]{3,2,1,0:T(1,128)S(1)}, u32[]{:S(2)}, u32[]{:S(2)}) %collective-permute-start.1) | collective-permute-done | bytes 81952 | tf_op jit(solution)/shard_map/ppermute | solution.py:37
  43.0 0.3 pad_maximum_fusion
  44.1 0.4 fusion.17
  45.1 0.3 multiply_add_fusion.5
  45.6 8.9 %collective-permute-start.7 = (f32[5,4,1,1024]{3,2,1,0:T(1,128)S(1)}, f32[5,4,1,1024]{3,2,1,0:T(1,128)S(1)}, u32[]{:S(2)}, u32[]{:S(2)}) collective-permute-start(f32[5,4,1,1024]{3,2,1,0:T(1,128)S(1)} %get-tuple-element.243), channel_id=1, source_target_pairs={{1,0},{2,1},{3,2},{4,3},{5,4},{6,5},{7,6},{8,7},{9,8},{10,9},{11,1... | collective-permute-start | bytes 245768 | tf_op jit(solution)/shard_map/ppermute | solution.py:37
  54.5 1.9 %collective-permute-done.6 = f32[5,4,1,1024]{3,2,1,0:T(1,128)S(1)} collective-permute-done((f32[5,4,1,1024]{3,2,1,0:T(1,128)S(1)}, f32[5,4,1,1024]{3,2,1,0:T(1,128)S(1)}, u32[]{:S(2)}, u32[]{:S(2)}) %collective-permute-start.6) | collective-permute-done | bytes 81952 | tf_op jit(solution)/shard_map/ppermute | solution.py:34
  56.5 0.4 collective-permute-done.7
  56.9 0.4 pad_maximum_fusion.1
  58.0 0.4 fusion.54
  59.1 0.3 multiply_add_fusion.4
  59.4 1.1 copy-done
  60.7 9.6 %collective-permute-start.9 = (f32[5,4,1,1024]{3,2,1,0:T(1,128)S(1)}, f32[5,4,1,1024]{3,2,1,0:T(1,128)S(1)}, u32[]{:S(2)}, u32[]{:S(2)}) collective-permute-start(f32[5,4,1,1024]{3,2,1,0:T(1,128)S(1)} %get-tuple-element.241), channel_id=1, source_target_pairs={{1,0},{2,1},{3,2},{4,3},{5,4},{6,5},{7,6},{8,7},{9,8},{10,9},{11,1... | collective-permute-start | bytes 245768 | tf_op jit(solution)/shard_map/ppermute | solution.py:37
  70.3 1.8 %collective-permute-done.8 = f32[5,4,1,1024]{3,2,1,0:T(1,128)S(1)} collective-permute-done((f32[5,4,1,1024]{3,2,1,0:T(1,128)S(1)}, f32[5,4,1,1024]{3,2,1,0:T(1,128)S(1)}, u32[]{:S(2)}, u32[]{:S(2)}) %collective-permute-start.8) | collective-permute-done | bytes 81952 | tf_op jit(solution)/shard_map/ppermute | solution.py:34
  72.1 1.6 %pad_maximum_fusion.2 = f32[5,4,18,1024]{3,2,1,0:T(8,128)S(1)} fusion(f32[5,4,1,1024]{3,2,1,0:T(1,128)S(1)} %collective-permute-done.9, f32[5,4,16,1024]{3,2,1,0:T(8,128)} %copy-done, f32[5,4,1,1024]{3,2,1,0:T(1,128)S(1)} %collective-permute-done.8), kind=kLoop, calls=%fused_computation.6 | loop fusion | flops 737280 | bytes 2949120 | tf_op jit(solution)/shard_map/concatenate | solution.py:38
  74.4 0.4 fusion.91
  75.4 0.3 multiply_add_fusion.3
  76.1 8.0 %collective-permute-start.11 = (f32[5,4,1,1024]{3,2,1,0:T(1,128)S(1)}, f32[5,4,1,1024]{3,2,1,0:T(1,128)S(1)}, u32[]{:S(2)}, u32[]{:S(2)}) collective-permute-start(f32[5,4,1,1024]{3,2,1,0:T(1,128)S(1)} %get-tuple-element.239), channel_id=1, source_target_pairs={{1,0},{2,1},{3,2},{4,3},{5,4},{6,5},{7,6},{8,7},{9,8},{10,9},{11,1... | collective-permute-start | bytes 245768 | tf_op jit(solution)/shard_map/ppermute | solution.py:37
  84.2 8.9 %all_gather.14 = f32[4,16,1024]{2,1,0:T(8,128)S(1)} all-gather(f32[1,16,1024]{2,1,0:T(8,128)S(1)} %slice.1009), channel_id=1, replica_groups=mesh['lev'=4,'row'=64] {'lev'}, dimensions={0}, use_global_device_ids=true | all-gather | bytes 327680 | tf_op jit(solution)/shard_map/all_gather | solution.py:18
  93.4 1.0 fusion.301
  94.4 5.9 %all_gather.15 = f32[4,16,1024]{2,1,0:T(8,128)S(1)} all-gather(f32[1,16,1024]{2,1,0:T(8,128)S(1)} %slice.1010), channel_id=1, replica_groups=mesh['lev'=4,'row'=64] {'lev'}, dimensions={0}, use_global_device_ids=true | all-gather | bytes 327680 | tf_op jit(solution)/shard_map/all_gather | solution.py:18
  100.4 2.8 %collective-permute-start.12 = (f32[4,1,1024]{2,1,0:T(1,128)S(1)}, f32[4,1,1024]{2,1,0:T(1,128)S(1)}, u32[]{:S(2)}, u32[]{:S(2)}) collective-permute-start(f32[4,1,1024]{2,1,0:T(1,128)S(1)} %get-tuple-element.260), channel_id=1, source_target_pairs={{1,0},{2,1},{3,2},{4,3},{5,4},{6,5},{7,6},{8,7},{9,8},{10,9},{11,1... | collective-permute-start | bytes 49160 | tf_op jit(solution)/shard_map/ppermute | solution.py:37
  103.2 0.3 pad_maximum_fusion.3
  104.1 8.0 %collective-permute-done.13 = f32[4,1,1024]{2,1,0:T(1,128)S(1)} collective-permute-done((f32[4,1,1024]{2,1,0:T(1,128)S(1)}, f32[4,1,1024]{2,1,0:T(1,128)S(1)}, u32[]{:S(2)}, u32[]{:S(2)}) %collective-permute-start.13) | collective-permute-done | bytes 16416 | tf_op jit(solution)/shard_map/ppermute | solution.py:34
  112.4 0.4 fusion.128
  113.4 0.3 multiply_add_fusion.2
  113.9 7.8 %collective-permute-start.15 = (f32[5,4,1,1024]{3,2,1,0:T(1,128)S(1)}, f32[5,4,1,1024]{3,2,1,0:T(1,128)S(1)}, u32[]{:S(2)}, u32[]{:S(2)}) collective-permute-start(f32[5,4,1,1024]{3,2,1,0:T(1,128)S(1)} %get-tuple-element.237), channel_id=1, source_target_pairs={{1,0},{2,1},{3,2},{4,3},{5,4},{6,5},{7,6},{8,7},{9,8},{10,9},{11,1... | collective-permute-start | bytes 245768 | tf_op jit(solution)/shard_map/ppermute | solution.py:37
  121.7 1.8 %collective-permute-done.14 = f32[5,4,1,1024]{3,2,1,0:T(1,128)S(1)} collective-permute-done((f32[5,4,1,1024]{3,2,1,0:T(1,128)S(1)}, f32[5,4,1,1024]{3,2,1,0:T(1,128)S(1)}, u32[]{:S(2)}, u32[]{:S(2)}) %collective-permute-start.14) | collective-permute-done | bytes 81952 | tf_op jit(solution)/shard_map/ppermute | solution.py:34
  123.7 0.4 pad_maximum_fusion.4
  124.6 0.3 fusion.156
  124.9 0.4 fusion.165
  125.9 0.3 multiply_add_fusion.1
  126.4 8.3 %collective-permute-start.17 = (f32[5,4,1,1024]{3,2,1,0:T(1,128)S(1)}, f32[5,4,1,1024]{3,2,1,0:T(1,128)S(1)}, u32[]{:S(2)}, u32[]{:S(2)}) collective-permute-start(f32[5,4,1,1024]{3,2,1,0:T(1,128)S(1)} %get-tuple-element.235), channel_id=1, source_target_pairs={{1,0},{2,1},{3,2},{4,3},{5,4},{6,5},{7,6},{8,7},{9,8},{10,9},{11,1... | collective-permute-start | bytes 245768 | tf_op jit(solution)/shard_map/ppermute | solution.py:37
  134.7 2.6 %collective-permute-done.16 = f32[5,4,1,1024]{3,2,1,0:T(1,128)S(1)} collective-permute-done((f32[5,4,1,1024]{3,2,1,0:T(1,128)S(1)}, f32[5,4,1,1024]{3,2,1,0:T(1,128)S(1)}, u32[]{:S(2)}, u32[]{:S(2)}) %collective-permute-start.16) | collective-permute-done | bytes 81952 | tf_op jit(solution)/shard_map/ppermute | solution.py:34
  137.4 0.4 pad_maximum_fusion.5
  138.5 0.4 fusion.202
  139.5 0.3 multiply_add_fusion
  139.8 1.1 slice_bitcast_fusion.30
  (141 shorter events, 10.6 us)
Async XLA Ops:
  0.6 20.0 %copy-start.9 = (f32[16]{0:T(128)S(1)}, f32[16]{0:T(128)}, u32[]{:S(2)}) copy-start(f32[16]{0:T(128)} %param.22) | copy-start | bytes 196
  1.4 30.4 %collective-permute-start.4 = (f32[1,1024]{1,0:T(1,128)S(1)}, f32[1,1024]{1,0:T(1,128)S(1)}, u32[]{:S(2)}, u32[]{:S(2)}) collective-permute-start(f32[1,1024]{1,0:T(1,128)S(1)} %get-tuple-element.269), channel_id=1, source_target_pairs={{0,1},{1,2},{2,3},{3,4},{4,5},{5,6},{6,7},{7,8},{8,9},{9,10},{10,1... | collective-permute-start | bytes 12296 | tf_op jit(solution)/shard_map/ppermute | solution.py:34
  5.2 34.5 %collective-permute-start.5 = (f32[1,1024]{1,0:T(1,128)S(1)}, f32[1,1024]{1,0:T(1,128)S(1)}, u32[]{:S(2)}, u32[]{:S(2)}) collective-permute-start(f32[1,1024]{1,0:T(1,128)S(1)} %get-tuple-element.270), channel_id=1, source_target_pairs={{1,0},{2,1},{3,2},{4,3},{5,4},{6,5},{7,6},{8,7},{9,8},{10,9},{11,1... | collective-permute-start | bytes 12296 | tf_op jit(solution)/shard_map/ppermute | solution.py:37
  20.9 7.2 %copy-start.3 = (f32[16,1024]{1,0:T(8,128)S(1)}, f32[16,1024]{1,0:T(8,128)}, u32[]{:S(2)}) copy-start(f32[16,1024]{1,0:T(8,128)} %param.23) | copy-start | bytes 196612
  21.9 8.9 %copy-start.4 = (f32[4,16,1024]{2,1,0:T(8,128)S(1)}, f32[4,16,1024]{2,1,0:T(8,128)}, u32[]{:S(2)}) copy-start(f32[4,16,1024]{2,1,0:T(8,128)} %param.17) | copy-start | bytes 786436
  27.9 2.9 %copy-start.5 = (f32[4,16,1024]{2,1,0:T(8,128)S(1)}, f32[4,16,1024]{2,1,0:T(8,128)}, u32[]{:S(2)}) copy-start(f32[4,16,1024]{2,1,0:T(8,128)} %param.18) | copy-start | bytes 786436
  27.9 2.9 %copy-start.2 = (f32[4,16,1024]{2,1,0:T(8,128)S(1)}, f32[4,16,1024]{2,1,0:T(8,128)}, u32[]{:S(2)}) copy-start(f32[4,16,1024]{2,1,0:T(8,128)} %param.19) | copy-start | bytes 786436
  28.0 2.9 %copy-start.6 = (f32[4,16,1024]{2,1,0:T(8,128)S(1)}, f32[4,16,1024]{2,1,0:T(8,128)}, u32[]{:S(2)}) copy-start(f32[4,16,1024]{2,1,0:T(8,128)} %param.20) | copy-start | bytes 786436
  28.1 2.9 %copy-start.7 = (f32[4,16,1024]{2,1,0:T(8,128)S(1)}, f32[4,16,1024]{2,1,0:T(8,128)}, u32[]{:S(2)}) copy-start(f32[4,16,1024]{2,1,0:T(8,128)} %param.21) | copy-start | bytes 786436
  28.1 15.6 %collective-permute-start.2 = (f32[4,1,1024]{2,1,0:T(1,128)S(1)}, f32[4,1,1024]{2,1,0:T(1,128)S(1)}, u32[]{:S(2)}, u32[]{:S(2)}) collective-permute-start(f32[4,1,1024]{2,1,0:T(1,128)S(1)} %get-tuple-element.264), channel_id=1, source_target_pairs={{1,0},{2,1},{3,2},{4,3},{5,4},{6,5},{7,6},{8,7},{9,8},{10,9},{11,1... | collective-permute-start | bytes 49160 | tf_op jit(solution)/shard_map/ppermute | solution.py:37
  30.8 13.0 %collective-permute-start.3 = (f32[4,1,1024]{2,1,0:T(1,128)S(1)}, f32[4,1,1024]{2,1,0:T(1,128)S(1)}, u32[]{:S(2)}, u32[]{:S(2)}) collective-permute-start(f32[4,1,1024]{2,1,0:T(1,128)S(1)} %get-tuple-element.265), channel_id=1, source_target_pairs={{0,1},{1,2},{2,3},{3,4},{4,5},{5,6},{6,7},{7,8},{8,9},{9,10},{10,1... | collective-permute-start | bytes 49160 | tf_op jit(solution)/shard_map/ppermute | solution.py:34
  30.8 0.8 copy-start.1
  30.8 0.9 copy-start.8
  31.1 10.2 %collective-permute-start = (f32[5,4,1,1024]{3,2,1,0:T(1,128)S(1)}, f32[5,4,1,1024]{3,2,1,0:T(1,128)S(1)}, u32[]{:S(2)}, u32[]{:S(2)}) collective-permute-start(f32[5,4,1,1024]{3,2,1,0:T(1,128)S(1)} %get-tuple-element.244), channel_id=1, source_target_pairs={{0,1},{1,2},{2,3},{3,4},{4,5},{5,6},{6,7},{7,8},{8,9},{9,10},{10,1... | collective-permute-start | bytes 245768 | tf_op jit(solution)/shard_map/ppermute | solution.py:34
  31.9 11.2 %collective-permute-start.1 = (f32[5,4,1,1024]{3,2,1,0:T(1,128)S(1)}, f32[5,4,1,1024]{3,2,1,0:T(1,128)S(1)}, u32[]{:S(2)}, u32[]{:S(2)}) collective-permute-start(f32[5,4,1,1024]{3,2,1,0:T(1,128)S(1)} %get-tuple-element.245), channel_id=1, source_target_pairs={{1,0},{2,1},{3,2},{4,3},{5,4},{6,5},{7,6},{8,7},{9,8},{10,9},{11,1... | collective-permute-start | bytes 245768 | tf_op jit(solution)/shard_map/ppermute | solution.py:37
  45.5 11.0 %collective-permute-start.6 = (f32[5,4,1,1024]{3,2,1,0:T(1,128)S(1)}, f32[5,4,1,1024]{3,2,1,0:T(1,128)S(1)}, u32[]{:S(2)}, u32[]{:S(2)}) collective-permute-start(f32[5,4,1,1024]{3,2,1,0:T(1,128)S(1)} %get-tuple-element.242), channel_id=1, source_target_pairs={{0,1},{1,2},{2,3},{3,4},{4,5},{5,6},{6,7},{7,8},{8,9},{9,10},{10,1... | collective-permute-start | bytes 245768 | tf_op jit(solution)/shard_map/ppermute | solution.py:34
  45.6 11.3 %collective-permute-start.7 = (f32[5,4,1,1024]{3,2,1,0:T(1,128)S(1)}, f32[5,4,1,1024]{3,2,1,0:T(1,128)S(1)}, u32[]{:S(2)}, u32[]{:S(2)}) collective-permute-start(f32[5,4,1,1024]{3,2,1,0:T(1,128)S(1)} %get-tuple-element.243), channel_id=1, source_target_pairs={{1,0},{2,1},{3,2},{4,3},{5,4},{6,5},{7,6},{8,7},{9,8},{10,9},{11,1... | collective-permute-start | bytes 245768 | tf_op jit(solution)/shard_map/ppermute | solution.py:37
  59.4 1.1 copy-start
  60.6 11.5 %collective-permute-start.8 = (f32[5,4,1,1024]{3,2,1,0:T(1,128)S(1)}, f32[5,4,1,1024]{3,2,1,0:T(1,128)S(1)}, u32[]{:S(2)}, u32[]{:S(2)}) collective-permute-start(f32[5,4,1,1024]{3,2,1,0:T(1,128)S(1)} %get-tuple-element.240), channel_id=1, source_target_pairs={{0,1},{1,2},{2,3},{3,4},{4,5},{5,6},{6,7},{7,8},{8,9},{9,10},{10,1... | collective-permute-start | bytes 245768 | tf_op jit(solution)/shard_map/ppermute | solution.py:34
  60.7 11.4 %collective-permute-start.9 = (f32[5,4,1,1024]{3,2,1,0:T(1,128)S(1)}, f32[5,4,1,1024]{3,2,1,0:T(1,128)S(1)}, u32[]{:S(2)}, u32[]{:S(2)}) collective-permute-start(f32[5,4,1,1024]{3,2,1,0:T(1,128)S(1)} %get-tuple-element.241), channel_id=1, source_target_pairs={{1,0},{2,1},{3,2},{4,3},{5,4},{6,5},{7,6},{8,7},{9,8},{10,9},{11,1... | collective-permute-start | bytes 245768 | tf_op jit(solution)/shard_map/ppermute | solution.py:37
  76.0 27.1 %collective-permute-start.10 = (f32[5,4,1,1024]{3,2,1,0:T(1,128)S(1)}, f32[5,4,1,1024]{3,2,1,0:T(1,128)S(1)}, u32[]{:S(2)}, u32[]{:S(2)}) collective-permute-start(f32[5,4,1,1024]{3,2,1,0:T(1,128)S(1)} %get-tuple-element.238), channel_id=1, source_target_pairs={{0,1},{1,2},{2,3},{3,4},{4,5},{5,6},{6,7},{7,8},{8,9},{9,10},{10,1... | collective-permute-start | bytes 245768 | tf_op jit(solution)/shard_map/ppermute | solution.py:34
  76.1 27.1 %collective-permute-start.11 = (f32[5,4,1,1024]{3,2,1,0:T(1,128)S(1)}, f32[5,4,1,1024]{3,2,1,0:T(1,128)S(1)}, u32[]{:S(2)}, u32[]{:S(2)}) collective-permute-start(f32[5,4,1,1024]{3,2,1,0:T(1,128)S(1)} %get-tuple-element.239), channel_id=1, source_target_pairs={{1,0},{2,1},{3,2},{4,3},{5,4},{6,5},{7,6},{8,7},{9,8},{10,9},{11,1... | collective-permute-start | bytes 245768 | tf_op jit(solution)/shard_map/ppermute | solution.py:37
  100.4 3.6 %collective-permute-start.12 = (f32[4,1,1024]{2,1,0:T(1,128)S(1)}, f32[4,1,1024]{2,1,0:T(1,128)S(1)}, u32[]{:S(2)}, u32[]{:S(2)}) collective-permute-start(f32[4,1,1024]{2,1,0:T(1,128)S(1)} %get-tuple-element.260), channel_id=1, source_target_pairs={{1,0},{2,1},{3,2},{4,3},{5,4},{6,5},{7,6},{8,7},{9,8},{10,9},{11,1... | collective-permute-start | bytes 49160 | tf_op jit(solution)/shard_map/ppermute | solution.py:37
  103.2 8.9 %collective-permute-start.13 = (f32[4,1,1024]{2,1,0:T(1,128)S(1)}, f32[4,1,1024]{2,1,0:T(1,128)S(1)}, u32[]{:S(2)}, u32[]{:S(2)}) collective-permute-start(f32[4,1,1024]{2,1,0:T(1,128)S(1)} %get-tuple-element.261), channel_id=1, source_target_pairs={{0,1},{1,2},{2,3},{3,4},{4,5},{5,6},{6,7},{7,8},{8,9},{9,10},{10,1... | collective-permute-start | bytes 49160 | tf_op jit(solution)/shard_map/ppermute | solution.py:34
  113.8 9.7 %collective-permute-start.14 = (f32[5,4,1,1024]{3,2,1,0:T(1,128)S(1)}, f32[5,4,1,1024]{3,2,1,0:T(1,128)S(1)}, u32[]{:S(2)}, u32[]{:S(2)}) collective-permute-start(f32[5,4,1,1024]{3,2,1,0:T(1,128)S(1)} %get-tuple-element.236), channel_id=1, source_target_pairs={{0,1},{1,2},{2,3},{3,4},{4,5},{5,6},{6,7},{7,8},{8,9},{9,10},{10,1... | collective-permute-start | bytes 245768 | tf_op jit(solution)/shard_map/ppermute | solution.py:34
  113.9 9.8 %collective-permute-start.15 = (f32[5,4,1,1024]{3,2,1,0:T(1,128)S(1)}, f32[5,4,1,1024]{3,2,1,0:T(1,128)S(1)}, u32[]{:S(2)}, u32[]{:S(2)}) collective-permute-start(f32[5,4,1,1024]{3,2,1,0:T(1,128)S(1)} %get-tuple-element.237), channel_id=1, source_target_pairs={{1,0},{2,1},{3,2},{4,3},{5,4},{6,5},{7,6},{8,7},{9,8},{10,9},{11,1... | collective-permute-start | bytes 245768 | tf_op jit(solution)/shard_map/ppermute | solution.py:37
  126.3 11.0 %collective-permute-start.16 = (f32[5,4,1,1024]{3,2,1,0:T(1,128)S(1)}, f32[5,4,1,1024]{3,2,1,0:T(1,128)S(1)}, u32[]{:S(2)}, u32[]{:S(2)}) collective-permute-start(f32[5,4,1,1024]{3,2,1,0:T(1,128)S(1)} %get-tuple-element.234), channel_id=1, source_target_pairs={{0,1},{1,2},{2,3},{3,4},{4,5},{5,6},{6,7},{7,8},{8,9},{9,10},{10,1... | collective-permute-start | bytes 245768 | tf_op jit(solution)/shard_map/ppermute | solution.py:34
  126.4 11.0 %collective-permute-start.17 = (f32[5,4,1,1024]{3,2,1,0:T(1,128)S(1)}, f32[5,4,1,1024]{3,2,1,0:T(1,128)S(1)}, u32[]{:S(2)}, u32[]{:S(2)}) collective-permute-start(f32[5,4,1,1024]{3,2,1,0:T(1,128)S(1)} %get-tuple-element.235), channel_id=1, source_target_pairs={{1,0},{2,1},{3,2},{4,3},{5,4},{6,5},{7,6},{8,7},{9,8},{10,9},{11,1... | collective-permute-start | bytes 245768 | tf_op jit(solution)/shard_map/ppermute | solution.py:37
where the time goes:
time: 142 us; the launch traced here: 141 us
  starting transfers between devices  68 us (48%)
  blocking collectives  27.4 us (19%)
  waiting for transfers between devices  20.3 us (14%)
  other arithmetic  17.5 us (12%)
  local copies, waits for them, and re-layouts  6.05 us (4%)
  between operations  1.55 us (1%)
    ppermute x9, starting transfers between devices, extended(): lax.ppermute(lax.slice_in_dim(block, 0, width, axis=dim), axis, backward)  63.7 us
    all_gather x4, blocking collectives, carried_in(): gathered = lax.all_gather(part, axis)  27.4 us
    ppermute x9, waiting for transfers between devices, extended(): lax.ppermute(lax.slice_in_dim(block, block.shape[dim] - width, None, axis...  17.8 us
    unnamed x24, other arithmetic  6.39 us
    ppermute x9, starting transfers between devices, extended(): lax.ppermute(lax.slice_in_dim(block, block.shape[dim] - width, None, axis...  4.33 us
    concatenate x7, other arithmetic, extended(): block = jnp.concatenate([low, block, high], axis=dim)  3.45 us
  transfers between devices with their start and end apart: 18, of which 10 were waited for; matrix products, arithmetic and copies ran while one was open for 4% of the time, Pallas kernels for 0%

commit v1 on v0

v1 whole, which is shorter than its diff:
```python
import functools

import jax
import jax.numpy as jnp
from jax import lax
from jax.experimental import pallas as pl
from jax.experimental.pallas import tpu as pltpu
from jax.sharding import PartitionSpec as P

OUTER = 2
SECTIONS = (1.0 / 3.0, 0.5, 1.0)

time_step = 0.05
top_pressure = 0.1
exner_power = 2.0 / 7.0

MESH = pl.DeviceIdType.MESH
VMEM = pltpu.VMEM

HALO = 3
OWN = 12
DEPTH = 40
LANES = 128
SUB = 8

TOTAL, PAIR, PAIR_UP, PAIR_DN, TOTAL_UP, TOTAL_DN = range(6)
EXNER, BELOW, BELOW_UP, BELOW_DN, EXNER_UP, EXNER_DN = range(6, 12)
MASS_UP, MASS_DN, WIND_UP, WIND_DN, TRACE_UP, TRACE_DN, PLANE_UP, PLANE_DN = range(12, 20)
MESSAGES = 20


def column_gap(a, edge=False):
    lane = lax.broadcasted_iota(jnp.int32, (1,) + a.shape[1:], 2)
    low, high = (a[:1], a[-1:]) if edge else (jnp.zeros_like(a[:1]), jnp.zeros_like(a[:1]))
    east = pltpu.roll(a, LANES - 1, 2)
    west = pltpu.roll(a, 1, 2)
    east = jnp.where(lane == LANES - 1, jnp.concatenate([east[1:], high], 0), east)
    west = jnp.where(lane == 0, jnp.concatenate([low, west[:-1]], 0), west)
    return east - west


def steps_kernel(
    levels,
    columns,
    row_devices,
    east_in,
    north_in,
    mass_in,
    one_in,
    two_in,
    theta,
    geopot_in,
    metric_in,
    active_in,
    east_out,
    north_out,
    mass_out,
    one_out,
    two_out,
    state,
    first,
    second,
    planes,
    active_raw,
    total,
    total_pair,
    pair,
    above,
    exner,
    exner_pair,
    low_pair,
    below,
    weight,
    potential,
    slope_x,
    slope_y,
    half_metric,
    half_square,
    spin,
    inverse,
    load_sem,
    send_sem,
    recv_sem,
):
    layers, blocks = state.shape[2], state.shape[3]
    lev, row = lax.axis_index("lev"), lax.axis_index("row")
    up_row = lax.rem(row + 1, row_devices)
    dn_row = lax.rem(row + row_devices - 1, row_devices)
    odd = lax.rem(lev, 2)
    core = (lev + 1 - 2 * odd, row)
    far_lev = lax.rem(lev + 2, 4)
    far, far_up, far_dn = (far_lev, row), (far_lev, up_row), (far_lev, dn_row)
    up, dn = (lev, up_row), (lev, dn_row)
    is_odd, is_even = odd == 1, odd == 0
    is_high, is_low = lev < 2, lev >= 2
    own = pl.ds(OWN, 2 * SUB)
    first_layer = lev * layers

    def load(slot, source, target):
        return [
            pltpu.make_async_copy(
                source(half), target(pl.ds(OWN + half * SUB, SUB)), load_sem.at[slot, half]
            )
            for half in range(2)
        ]

    def load_field(slot, ref, field):
        return load(slot, lambda half: ref.at[:, half], lambda rows: state.at[0, field, :, :, rows, :])

    loads_mass = load_field(0, mass_in, 2)
    loads_planes = (
        load(1, lambda half: metric_in.at[half], lambda rows: planes.at[0, :, rows, :])
        + load(2, lambda half: geopot_in.at[half], lambda rows: planes.at[1, :, rows, :])
        + load(3, lambda half: active_in.at[half], lambda rows: active_raw.at[:, rows, :])
    )
    loads_wind = load_field(4, east_in, 0) + load_field(5, north_in, 1)
    loads_trace = load_field(6, one_in, 3) + load_field(7, two_in, 4)
    for copy in loads_mass + loads_planes + loads_wind + loads_trace:
        copy.start()

    barrier = pltpu.get_barrier_semaphore()
    for device in (core, far, up, dn, far_up, far_dn):
        pl.semaphore_signal(barrier, inc=1, device_id=device, device_id_type=MESH)

    def message(outer, kind, source, target, device):
        return pltpu.make_async_remote_copy(
            src_ref=source,
            dst_ref=target,
            send_sem=send_sem.at[outer, kind],
            recv_sem=recv_sem.at[outer, kind],
            device_id=device,
            device_id_type=MESH,
        )

    edge_up = (pl.ds(OWN + 2 * SUB - HALO, HALO), pl.ds(OWN - HALO, HALO))
    edge_dn = (pl.ds(OWN, HALO), pl.ds(OWN + 2 * SUB, HALO))

    def edges(outer, kinds, ref, ref_to, to_up, to_dn):
        return [
            message(outer, kind, ref(rows[0]), ref_to(rows[1]), device)
            for kind, rows, device in zip(kinds, (edge_up, edge_dn), (to_up, to_dn))
        ]

    def plane_rows(ref, outer):
        return lambda rows: ref.at[outer, :, rows, :]

    def field_rows(outer, field, count):
        return lambda rows: state.at[outer, pl.ds(field, count), :, :, rows, :]

    def all_messages(outer):
        same = lambda kinds, ref: edges(outer, kinds, ref, ref, up, dn)
        msg = {}
        msg["total"] = [message(outer, TOTAL, total.at[outer, :, own, :], total_pair.at[outer, :, own, :], core)]
        msg["pair"] = [
            message(outer, PAIR, pair.at[outer, :, own, :], above.at[outer, :, own, :], far)
        ]
        msg["pair_edge"] = edges(
            outer, (PAIR_UP, PAIR_DN), plane_rows(pair, outer), plane_rows(above, outer), far_up, far_dn
        )
        msg["total_edge"] = same((TOTAL_UP, TOTAL_DN), plane_rows(total_pair, outer))
        msg["exner"] = [message(outer, EXNER, exner.at[outer, :, own, :], exner_pair.at[outer, :, own, :], core)]
        msg["below"] = [
            message(outer, BELOW, low_pair.at[outer, :, own, :], below.at[outer, :, own, :], far)
        ]
        msg["below_edge"] = edges(
            outer, (BELOW_UP, BELOW_DN), plane_rows(low_pair, outer), plane_rows(below, outer), far_up, far_dn
        )
        msg["exner_edge"] = same((EXNER_UP, EXNER_DN), plane_rows(exner_pair, outer))
        msg["mass"] = same((MASS_UP, MASS_DN), field_rows(outer, 2, 1))
        msg["wind"] = same((WIND_UP, WIND_DN), field_rows(outer, 0, 2))
        msg["trace"] = same((TRACE_UP, TRACE_DN), field_rows(outer, 3, 2))
        if outer == 0:
            msg["plane"] = same((PLANE_UP, PLANE_DN), lambda rows: planes.at[:, :, rows, :])
        return msg

    def start(copies):
        for copy in copies:
            copy.start()

    def arrive(copies):
        for copy in copies:
            copy.wait_recv()

    def sent(copies):
        for copy in copies:
            copy.wait_send()

    def tiles(count, body, unroll=1):
        def one(index, carry):
            body(index)
            return carry

        lax.fori_loop(0, count, one, 0, unroll=unroll)

    def sum_layers(outer):
        def body(tile):
            rows = pl.ds(OWN + SUB * tile, SUB)
            acc = jnp.abs(state[outer, 2, 0, :, rows, :])
            for layer in range(1, layers):
                acc = acc + jnp.abs(state[outer, 2, layer, :, rows, :])
            total[outer, :, rows, :] = acc

        tiles(2, body, 2)

    def add_planes(outer, out, one, other):
        def body(tile):
            rows = pl.ds(OWN + SUB * tile, SUB)
            out[outer, :, rows, :] = one[outer, :, rows, :] + other[outer, :, rows, :]

        tiles(2, body, 2)

    def weigh(outer, starts, keep_sum):
        base, stride = starts

        def body(tile):
            rows = pl.ds(base + stride * tile, SUB)
            running = jnp.where(is_odd, total_pair[outer, :, rows, :], 0.0) + jnp.where(
                is_low, above[outer, :, rows, :], 0.0
            )
            weighted = []
            for layer in range(layers):
                running = running + jnp.abs(state[outer, 2, layer, :, rows, :])
                pressure = top_pressure + running * (1.0 / levels)
                weighted.append(theta[first_layer + layer] * jnp.exp(exner_power * jnp.log(pressure)))
            acc = weighted[-1]
            weight[layers - 1, :, rows, :] = acc
            for layer in range(layers - 2, -1, -1):
                acc = acc + weighted[layer]
                weight[layer, :, rows, :] = acc
            if keep_sum:
                exner[outer, :, rows, :] = acc

        tiles(2, body)

    def coefficients(starts):
        base, stride = starts
        shape = (blocks, SUB, LANES)
        column = LANES * lax.broadcasted_iota(jnp.int32, shape, 0) + lax.broadcasted_iota(jnp.int32, shape, 2)
        coriolis = 0.5 + column.astype(jnp.float32) / columns

        def body(tile):
            rows = pl.ds(base + stride * tile, SUB)
            metric = planes[0, :, rows, :]
            count = planes[2, :, rows, :]
            inverse[:, rows, :] = 1.0 / metric
            half = 0.5 * metric
            square = half * metric
            for layer in range(layers):
                active = count > (first_layer + layer).astype(jnp.float32)
                half_metric[layer, :, rows, :] = jnp.where(active, half, 0.0)
                half_square[layer, :, rows, :] = jnp.where(active, square, 0.0)
                spin[layer, :, rows, :] = jnp.where(active, coriolis, 0.0)

        tiles(2, body)

    def montgomery(outer):
        def body(tile):
            rows = pl.ds(OWN - 4 + SUB * tile, SUB)
            rest = (
                planes[1, :, rows, :]
                + jnp.where(is_even, exner_pair[outer, :, rows, :], 0.0)
                + jnp.where(is_high, below[outer, :, rows, :], 0.0)
            )
            for layer in range(layers):
                potential[layer, :, rows, :] = rest + weight[layer, :, rows, :]

        tiles(3, body, 3)

        def slopes(index):
            layer, tile = index // 3, lax.rem(index, 3)
            base = OWN - 4 + SUB * tile
            rows = pl.ds(base, SUB)
            half = half_metric[layer, :, rows, :]
            slope_x[layer, :, rows, :] = half * (
                potential[layer, :, pl.ds(base + 1, SUB), :] - potential[layer, :, pl.ds(base - 1, SUB), :]
            )
            slope_y[layer, :, rows, :] = half * column_gap(potential[layer, :, rows, :], edge=True)

        tiles(3 * layers, slopes, 4)

    def section(outer, number, fields, results):
        count = 2 if number == 2 else 3
        begin = OWN if number == 2 else OWN - 4
        factor = time_step * SECTIONS[number]
        source = (state.at[outer], first, second)[number]

        def body(index):
            layer, tile = index // count, lax.rem(index, count)
            base = begin + SUB * tile

            def get(ref, field, shift=0):
                return ref[field, layer, :, pl.ds(base + shift, SUB), :]

            def plane(ref):
                return ref[layer, :, pl.ds(base, SUB), :]

            start_of = state.at[outer]
            half = plane(half_metric) * factor
            east, north = get(source, 0), get(source, 1)
            flow_x, flow_y = half * east, half * north

            def carried(field):
                middle = get(source, field)
                return flow_x * (get(source, field, 1) - get(source, field, -1)) + flow_y * column_gap(middle)

            if 0 in fields:
                turn = plane(spin) * factor
                results(0, layer, tile)[...] = (
                    get(start_of, 0) + (turn * north - plane(slope_x) * factor) - carried(0)
                )
                results(1, layer, tile)[...] = (
                    get(start_of, 1) - (turn * east + plane(slope_y) * factor) - carried(1)
                )

                def flux(shift):
                    return get(source, 2, shift) * get(source, 0, shift) * inverse[:, pl.ds(base + shift, SUB), :]

                across = get(source, 2) * north * plane_of(inverse, base)
                results(2, layer, tile)[...] = get(start_of, 2) - factor * plane(half_square) * (
                    (flux(1) - flux(-1)) + column_gap(across)
                )
            if 3 in fields:
                for field in (3, 4):
                    results(field, layer, tile)[...] = get(start_of, field) - carried(field)

        tiles(count * layers, body, 4)

    def plane_of(ref, base):
        return ref[:, pl.ds(base, SUB), :]

    outputs = (east_out, north_out, mass_out, one_out, two_out)

    def results_of(outer, number):
        if number < 2:
            ref = (first, second)[number]
            return lambda field, layer, tile: ref.at[field, layer, :, pl.ds(OWN - 4 + SUB * tile, SUB), :]
        if outer + 1 < OUTER:
            return lambda field, layer, tile: state.at[outer + 1, field, layer, :, pl.ds(OWN + SUB * tile, SUB), :]
        return lambda field, layer, tile: outputs[field].at[layer, :, pl.ds(SUB * tile, SUB), :]

    DYNAMICS, TRACERS = (0, 1, 2), (3, 4)

    def run(outer, number, fields):
        section(outer, number, fields, results_of(outer, number))

    inner = (OWN, SUB)
    outer_rows = (OWN - SUB, 3 * SUB)
    sends = []
    high_sends, low_sends, odd_sends, even_sends = [], [], [], []

    previous = None
    for outer in range(OUTER):
        msg = all_messages(outer)
        if outer == 0:
            for copy in loads_mass:
                copy.wait()
            sum_layers(outer)
            pl.semaphore_wait(barrier, 6)
            start(msg["total"])
            start(msg["mass"])
            for copy in loads_planes:
                copy.wait()

            def count_up(tile):
                rows = pl.ds(OWN + SUB * tile, SUB)
                planes[2, :, rows, :] = active_raw[:, rows, :].astype(jnp.float32)

            tiles(2, count_up)
            start(msg["plane"])
            sends += msg["plane"]
            for copy in loads_wind:
                copy.wait()
            start(msg["wind"])
        else:
            sum_layers(outer)
            start(msg["total"])
            start(msg["mass"])
            start(msg["wind"])
            arrive(previous["trace"])
            run(outer - 1, 0, TRACERS)
        sends += msg["total"] + msg["mass"] + msg["wind"]

        arrive(msg["total"])
        add_planes(outer, pair, total, total_pair)

        @pl.when(is_high)
        def _():
            start(msg["pair"])
            start(msg["pair_edge"])

        @pl.when(is_odd)
        def _():
            start(msg["total_edge"])

        high_sends += msg["pair"] + msg["pair_edge"]
        odd_sends += msg["total_edge"]

        if outer == 0:
            coefficients(inner)
            for copy in loads_trace:
                copy.wait()
        else:
            run(outer - 1, 1, TRACERS)
            run(outer - 1, 2, TRACERS)

        @pl.when(is_low)
        def _():
            arrive(msg["pair"])

        weigh(outer, inner, True)
        start(msg["exner"])
        start(msg["trace"])
        sends += msg["exner"] + msg["trace"]
        arrive(msg["exner"])
        add_planes(outer, low_pair, exner, exner_pair)

        @pl.when(is_low)
        def _():
            start(msg["below"])
            start(msg["below_edge"])

        @pl.when(is_even)
        def _():
            start(msg["exner_edge"])

        low_sends += msg["below"] + msg["below_edge"]
        even_sends += msg["exner_edge"]

        if outer == 0:
            arrive(msg["plane"])
            coefficients(outer_rows)
        arrive(msg["mass"])

        @pl.when(is_odd)
        def _():
            arrive(msg["total_edge"])

        @pl.when(is_low)
        def _():
            arrive(msg["pair_edge"])

        weigh(outer, outer_rows, False)

        @pl.when(is_even)
        def _():
            arrive(msg["exner_edge"])

        @pl.when(is_high)
        def _():
            arrive(msg["below"])
            arrive(msg["below_edge"])

        montgomery(outer)
        arrive(msg["wind"])
        for number in range(3):
            run(outer, number, DYNAMICS)
        previous = msg

    arrive(previous["trace"])
    for number in range(3):
        run(OUTER - 1, number, TRACERS)

    sent(sends)
    for condition, copies in (
        (is_high, high_sends),
        (is_low, low_sends),
        (is_odd, odd_sends),
        (is_even, even_sends),
    ):

        @pl.when(condition)
        def _(copies=copies):
            sent(copies)


def store_kernel(*refs):
    count = (len(refs) - 1) // 2
    sem = refs[-1]
    copies = [
        pltpu.make_async_copy(
            refs[field].at[:, :, pl.ds(SUB * half, SUB), :], refs[count + field].at[:, half], sem.at[field, half]
        )
        for field in range(count)
        for half in range(2)
    ]
    for copy in copies:
        copy.start()
    for copy in copies:
        copy.wait()


def local(row_devices, levels, *arguments):
    fields, theta, maps = arguments[:5], arguments[5], arguments[6:]
    layers, rows, columns = fields[0].shape
    blocks = columns // LANES

    def cut(values):
        lead = values.shape[:-2]
        values = values.reshape(lead + (rows // SUB, SUB, blocks, LANES))
        return pltpu.with_memory_space_constraint(jnp.swapaxes(values, -3, -2), pltpu.HBM)

    def joined(values):
        return jnp.swapaxes(values, -3, -2).reshape(layers, rows, columns)

    anywhere = pl.BlockSpec(memory_space=pltpu.HBM)
    in_vmem = pl.BlockSpec(memory_space=VMEM)
    part = jax.ShapeDtypeStruct((layers, blocks, rows, LANES), jnp.float32)
    plane = VMEM((OUTER, blocks, DEPTH, LANES), jnp.float32)
    volume = VMEM((layers, blocks, DEPTH, LANES), jnp.float32)
    results = pl.pallas_call(
        functools.partial(steps_kernel, levels, columns, row_devices),
        name="layer_steps",
        out_shape=[part] * 5,
        in_specs=[anywhere] * 5 + [pl.BlockSpec(memory_space=pltpu.SMEM)] + [anywhere] * 3,
        out_specs=[in_vmem] * 5,
        scratch_shapes=[
            VMEM((OUTER, 5, layers, blocks, DEPTH, LANES), jnp.float32),
            VMEM((5, layers, blocks, DEPTH, LANES), jnp.float32),
            VMEM((5, layers, blocks, DEPTH, LANES), jnp.float32),
            VMEM((3, blocks, DEPTH, LANES), jnp.float32),
            VMEM((blocks, DEPTH, LANES), jnp.int32),
        ]
        + [plane] * 8
        + [volume] * 7
        + [
            VMEM((blocks, DEPTH, LANES), jnp.float32),
            pltpu.SemaphoreType.DMA((8, 2)),
            pltpu.SemaphoreType.DMA((OUTER, MESSAGES)),
            pltpu.SemaphoreType.DMA((OUTER, MESSAGES)),
        ],
        compiler_params=pltpu.CompilerParams(
            collective_id=0, has_side_effects=True, vmem_limit_bytes=48 * 2**20
        ),
    )(*[cut(values) for values in fields], pltpu.with_memory_space_constraint(theta, pltpu.HBM), *[cut(values) for values in maps])

    stored = pl.pallas_call(
        store_kernel,
        name="store_layers",
        out_shape=[jax.ShapeDtypeStruct((layers, rows // SUB, blocks, SUB, LANES), jnp.float32)] * 5,
        in_specs=[in_vmem] * 5,
        out_specs=[anywhere] * 5,
        scratch_shapes=[pltpu.SemaphoreType.DMA((5, 2))],
        compiler_params=pltpu.CompilerParams(vmem_limit_bytes=2**20),
    )(*results)
    return tuple(joined(values) for values in stored)


def solution(mesh):
    layered = P("lev", "row", None)
    flat = P("row", None)
    row_devices, lev_devices = mesh.shape["row"], mesh.shape["lev"]

    def whole(*arguments):
        levels = arguments[0].shape[0]
        return jax.shard_map(
            functools.partial(local, row_devices, levels),
            mesh=mesh,
            in_specs=(layered,) * 5 + (P(),) + (flat,) * 3,
            out_specs=(layered,) * 5,
            check_vma=False,
        )(*arguments)

    return whole
```

time: 142 us -> 60 us (0.42)
  starting transfers between devices: 68 us -> 0 us
  Pallas kernels: 0 us -> 59.3 us
  blocking collectives: 27.4 us -> 0 us
  waiting for transfers between devices: 20.3 us -> 0 us
  other arithmetic: 17.5 us -> 0 us
  local copies, waits for them, and re-layouts: 6.05 us -> 0 us
    ppermute x18 -> x0, starting transfers between devices: 68 us -> none  [the longest x9 63.7 us: extended(): lax.ppermute(lax.slice_in_dim(block, 0, width, axis=dim), axis, backward)]
    pallas_call x0 -> x2, Pallas kernels: none -> 59.3 us  [the longest x1 58.1 us: local(): pl.pallas_call(functools.partial(steps_kernel, levels, columns, row_devic...]
    all_gather x4 -> x0, blocking collectives: 27.4 us -> none  [carried_in(): gathered = lax.all_gather(part, axis)]
    ppermute x18 -> x0, waiting for transfers between devices: 20.3 us -> none  [the longest x9 17.8 us: extended(): lax.ppermute(lax.slice_in_dim(block, block.shape[dim] - width, None, axis...]
    unnamed x24 -> x0, other arithmetic: 6.39 us -> none
    another operation x10 -> x0, other arithmetic: 4.41 us -> none  [the longest x2 1.96 us: potential_field(): summed = jnp.flip(jnp.cumsum(jnp.flip(weighted, 0), axis=0), 0)]
    concatenate x7 -> x0, other arithmetic: 3.45 us -> none  [extended(): block = jnp.concatenate([low, block, high], axis=dim)]
    slice x33 -> x0, local copies, waits for them, and re-layouts: 2.21 us -> none  [the longest x7 1.52 us: extended(): lax.slice_in_dim(block, block.shape[dim] - width, None, axis=dim)]
  transfers between devices with their start and end apart: 18 -> 0, of which waited for: 10 -> 0; matrix products, arithmetic and copies ran while one was open for 4% -> 0% of each run, Pallas kernels for 0% -> 0%
where the time goes in v1:
time: 60 us; the launch traced here: 59.9 us
  Pallas kernels  59.3 us (99%)
  between operations  0.64 us (1%)
    pallas_call x1, Pallas kernels, local(): pl.pallas_call(functools.partial(steps_kernel, levels, columns, row_devic...  58.1 us

profile of v1, /device:TPU:1, one launch (start us, length us, event | category | flops | bytes accessed | tf_op | source)
XLA Modules:
  0.0 59.9 jit_solution(547373965605265930)
XLA Ops:
  0.6 58.1 %layer_steps.1 = (f32[4,8,16,128]{3,2,1,0:T(8,128)S(1)}, f32[4,8,16,128]{3,2,1,0:T(8,128)S(1)}, f32[4,8,16,128]{3,2,1,0:T(8,128)S(1)}, f32[4,8,16,128]{3,2,1,0:T(8,128)S(1)}, f32[4,8,16,128]{3,2,1,0:T(8,128)S(1)}) custom-call(f32[4,2,8,8,128]{4,3,2,1,0:T(8,128)} %bitcast.39, f32[4,2,8,8,128]{4,3,2,1,0:T(8,128)} %bitcast.40, f32[4,2,8,8,128]{4,3,2,1,0:T(8,128)} %bitcast.41, ...), custom_call_target="tpu_custom_call" | custom-call | tf_op jit(solution)/shard_map/layer_steps/pallas_call | solution.py:510
  58.8 1.1 %store_layers.1 = (f32[4,2,8,8,128]{4,3,2,1,0:T(8,128)}, f32[4,2,8,8,128]{4,3,2,1,0:T(8,128)}, f32[4,2,8,8,128]{4,3,2,1,0:T(8,128)}, f32[4,2,8,8,128]{4,3,2,1,0:T(8,128)}, f32[4,2,8,8,128]{4,3,2,1,0:T(8,128)}) custom-call(f32[4,8,16,128]{3,2,1,0:T(8,128)S(1)} %get-tuple-element.15.refs_0_, f32[4,8,16,128]{3,2,1,0:T(8,128)S(1)} %get-tuple-element.16.refs_1_, ...), custom_call_target="tpu_custom_call" | custom-call | tf_op jit(solution)/shard_map/store_layers/pallas_call | solution.py:536

commit v2 on v1

--- a/solution.py
+++ b/solution.py
@@ -17,6 +17,7 @@
 MESH = pl.DeviceIdType.MESH
 VMEM = pltpu.VMEM
 
+PERIOD = 64
 HALO = 3
 OWN = 12
 DEPTH = 40
@@ -25,8 +26,8 @@
 
 TOTAL, PAIR, PAIR_UP, PAIR_DN, TOTAL_UP, TOTAL_DN = range(6)
 EXNER, BELOW, BELOW_UP, BELOW_DN, EXNER_UP, EXNER_DN = range(6, 12)
-MASS_UP, MASS_DN, WIND_UP, WIND_DN, TRACE_UP, TRACE_DN, PLANE_UP, PLANE_DN = range(12, 20)
-MESSAGES = 20
+MASS_UP, MASS_DN, WIND_UP, WIND_DN, ONE_UP, ONE_DN, TWO_UP, TWO_DN, METRIC_UP, METRIC_DN, GROUND_UP, GROUND_DN = range(12, 24)
+MESSAGES = 24
 
 
 def column_gap(a, edge=False):
@@ -43,6 +44,7 @@
     levels,
     columns,
     row_devices,
+    period,
     east_in,
     north_in,
     mass_in,
@@ -118,9 +120,42 @@
     for copy in loads_mass + loads_planes + loads_wind + loads_trace:
         copy.start()
 
+    early = lax.rem(row, period) == 0
+    late = jnp.logical_not(early)
+    up_early, dn_early = lax.rem(up_row, period) == 0, lax.rem(dn_row, period) == 0
     barrier = pltpu.get_barrier_semaphore()
-    for device in (core, far, up, dn, far_up, far_dn):
-        pl.semaphore_signal(barrier, inc=1, device_id=device, device_id_type=MESH)
+
+    def greet(*devices):
+        for device in devices:
+            pl.semaphore_signal(barrier, inc=1, device_id=device, device_id_type=MESH)
+
+    greet(core, far)
+
+    @pl.when(late & jnp.logical_not(up_early))
+    def _():
+        greet(up, far_up)
+
+    @pl.when(late & jnp.logical_not(dn_early))
+    def _():
+        greet(dn, far_dn)
+
+    def meet():
+        @pl.when(early)
+        def _():
+            pl.semaphore_wait(barrier, 2)
+            greet(up, far_up, dn, far_dn)
+
+        @pl.when(late)
+        def _():
+            pl.semaphore_wait(barrier, 6)
+
+        @pl.when(late & up_early)
+        def _():
+            greet(up, far_up)
+
+        @pl.when(late & dn_early)
+        def _():
+            greet(dn, far_dn)
 
     def message(outer, kind, source, target, device):
         return pltpu.make_async_remote_copy(
@@ -166,11 +201,17 @@
             outer, (BELOW_UP, BELOW_DN), plane_rows(low_pair, outer), plane_rows(below, outer), far_up, far_dn
         )
         msg["exner_edge"] = same((EXNER_UP, EXNER_DN), plane_rows(exner_pair, outer))
-        msg["mass"] = same((MASS_UP, MASS_DN), field_rows(outer, 2, 1))
-        msg["wind"] = same((WIND_UP, WIND_DN), field_rows(outer, 0, 2))
-        msg["trace"] = same((TRACE_UP, TRACE_DN), field_rows(outer, 3, 2))
-        if outer == 0:
-            msg["plane"] = same((PLANE_UP, PLANE_DN), lambda rows: planes.at[:, :, rows, :])
+        for name, kinds, ref in (
+            ("mass", (MASS_UP, MASS_DN), field_rows(outer, 2, 1)),
+            ("wind", (WIND_UP, WIND_DN), field_rows(outer, 0, 2)),
+            ("one", (ONE_UP, ONE_DN), field_rows(outer, 3, 1)),
+            ("two", (TWO_UP, TWO_DN), field_rows(outer, 4, 1)),
+            ("metric", (METRIC_UP, METRIC_DN), lambda rows: planes.at[pl.ds(0, 1), :, rows, :]),
+            ("ground", (GROUND_UP, GROUND_DN), lambda rows: planes.at[pl.ds(1, 2), :, rows, :]),
+        ):
+            if name not in ("metric", "ground") or outer == 0:
+                msg[name] = same(kinds, ref)
+                msg[name + "_up"], msg[name + "_dn"] = msg[name][:1], msg[name][1:]
         return msg
 
     def start(copies):
@@ -202,10 +243,11 @@
 
         tiles(2, body, 2)
 
-    def add_planes(outer, out, one, other):
+    def add_planes(outer, out, one, other, ground=False):
         def body(tile):
             rows = pl.ds(OWN + SUB * tile, SUB)
-            out[outer, :, rows, :] = one[outer, :, rows, :] + other[outer, :, rows, :]
+            both = one[outer, :, rows, :] + other[outer, :, rows, :]
+            out[outer, :, rows, :] = both + planes[1, :, rows, :] if ground else both
 
         tiles(2, body, 2)
 
@@ -246,7 +288,7 @@
             half = 0.5 * metric
             square = half * metric
             for layer in range(layers):
-                active = count > (first_layer + layer).astype(jnp.float32)
+                active = jnp.logical_or(count > (first_layer + layer).astype(jnp.float32), is_high)
                 half_metric[layer, :, rows, :] = jnp.where(active, half, 0.0)
                 half_square[layer, :, rows, :] = jnp.where(active, square, 0.0)
                 spin[layer, :, rows, :] = jnp.where(active, coriolis, 0.0)
@@ -256,10 +298,8 @@
     def montgomery(outer):
         def body(tile):
             rows = pl.ds(OWN - 4 + SUB * tile, SUB)
-            rest = (
-                planes[1, :, rows, :]
-                + jnp.where(is_even, exner_pair[outer, :, rows, :], 0.0)
-                + jnp.where(is_high, below[outer, :, rows, :], 0.0)
+            rest = jnp.where(is_even, exner_pair[outer, :, rows, :], 0.0) + jnp.where(
+                is_high, below[outer, :, rows, :], planes[1, :, rows, :]
             )
             for layer in range(layers):
                 potential[layer, :, rows, :] = rest + weight[layer, :, rows, :]
@@ -271,10 +311,14 @@
             base = OWN - 4 + SUB * tile
             rows = pl.ds(base, SUB)
             half = half_metric[layer, :, rows, :]
-            slope_x[layer, :, rows, :] = half * (
+            along = half * (
                 potential[layer, :, pl.ds(base + 1, SUB), :] - potential[layer, :, pl.ds(base - 1, SUB), :]
             )
-            slope_y[layer, :, rows, :] = half * column_gap(potential[layer, :, rows, :], edge=True)
+            across = half * column_gap(potential[layer, :, rows, :], edge=True)
+            slope_x[layer, :, rows, :] = along
+            slope_y[layer, :, rows, :] = across
+            first[0, layer, :, rows, :] = first[0, layer, :, rows, :] - (time_step * SECTIONS[0]) * along
+            first[1, layer, :, rows, :] = first[1, layer, :, rows, :] - (time_step * SECTIONS[0]) * across
 
         tiles(3 * layers, slopes, 4)
 
@@ -305,12 +349,12 @@
 
             if 0 in fields:
                 turn = plane(spin) * factor
-                results(0, layer, tile)[...] = (
-                    get(start_of, 0) + (turn * north - plane(slope_x) * factor) - carried(0)
-                )
-                results(1, layer, tile)[...] = (
-                    get(start_of, 1) - (turn * east + plane(slope_y) * factor) - carried(1)
-                )
+                push_x, push_y = turn * north, turn * east
+                if number > 0:
+                    push_x = push_x - plane(slope_x) * factor
+                    push_y = push_y + plane(slope_y) * factor
+                results(0, layer, tile)[...] = get(start_of, 0) + push_x - carried(0)
+                results(1, layer, tile)[...] = get(start_of, 1) - push_y - carried(1)
 
                 def flux(shift):
                     return get(source, 2, shift) * get(source, 0, shift) * inverse[:, pl.ds(base + shift, SUB), :]
@@ -319,8 +363,8 @@
                 results(2, layer, tile)[...] = get(start_of, 2) - factor * plane(half_square) * (
                     (flux(1) - flux(-1)) + column_gap(across)
                 )
-            if 3 in fields:
-                for field in (3, 4):
+            for field in fields:
+                if field > 2:
                     results(field, layer, tile)[...] = get(start_of, field) - carried(field)
 
         tiles(count * layers, body, 4)
@@ -349,15 +393,27 @@
     high_sends, low_sends, odd_sends, even_sends = [], [], [], []
 
     previous = None
+    held_back = []
     for outer in range(OUTER):
         msg = all_messages(outer)
+
+        def to_rows(copies, condition=None, first_step=outer == 0):
+            allowed = condition
+            if first_step:
+                held_back.append((condition, copies))
+                allowed = late if condition is None else late & condition
+            if allowed is None:
+                start(copies)
+            else:
+                pl.when(allowed)(functools.partial(start, copies))
+
         if outer == 0:
             for copy in loads_mass:
                 copy.wait()
             sum_layers(outer)
-            pl.semaphore_wait(barrier, 6)
+            meet()
             start(msg["total"])
-            start(msg["mass"])
+            to_rows(msg["mass"])
             for copy in loads_planes:
                 copy.wait()
 
@@ -366,19 +422,19 @@
                 planes[2, :, rows, :] = active_raw[:, rows, :].astype(jnp.float32)
 
             tiles(2, count_up)
-            start(msg["plane"])
-            sends += msg["plane"]
+            to_rows(msg["metric_dn"])
+            to_rows(msg["ground_dn"], is_low)
+            sends += msg["metric"]
+            low_sends += msg["ground"]
             for copy in loads_wind:
                 copy.wait()
-            start(msg["wind"])
         else:
             sum_layers(outer)
             start(msg["total"])
-            start(msg["mass"])
-            start(msg["wind"])
-            arrive(previous["trace"])
+            to_rows(msg["mass"])
+            arrive(previous["one"] + previous["two"])
             run(outer - 1, 0, TRACERS)
-        sends += msg["total"] + msg["mass"] + msg["wind"]
+        sends += msg["total"] + msg["mass"] + msg["wind"] + msg["exner"] + msg["one"] + msg["two"]
 
         arrive(msg["total"])
         add_planes(outer, pair, total, total_pair)
@@ -386,14 +442,13 @@
         @pl.when(is_high)
         def _():
             start(msg["pair"])
-            start(msg["pair_edge"])
-
-        @pl.when(is_odd)
-        def _():
-            start(msg["total_edge"])
-
-        high_sends += msg["pair"] + msg["pair_edge"]
+
+        to_rows(msg["pair_edge"], is_high)
+        to_rows(msg["total_edge"], is_odd)
+
+        high_sends += msg["pair_edge"]
         odd_sends += msg["total_edge"]
+        to_rows(msg["wind_dn"])
 
         if outer == 0:
             coefficients(inner)
@@ -401,33 +456,54 @@
                 copy.wait()
         else:
             run(outer - 1, 1, TRACERS)
-            run(outer - 1, 2, TRACERS)
+
+        @pl.when(is_high)
+        def _():
+            sent(msg["pair"])
 
         @pl.when(is_low)
         def _():
             arrive(msg["pair"])
 
+        if outer == 0:
+            to_rows(msg["metric_up"])
+            to_rows(msg["ground_up"], is_low)
+        to_rows(msg["wind_up"])
         weigh(outer, inner, True)
         start(msg["exner"])
-        start(msg["trace"])
-        sends += msg["exner"] + msg["trace"]
+        if outer > 0:
+            run(outer - 1, 2, TRACERS)
         arrive(msg["exner"])
-        add_planes(outer, low_pair, exner, exner_pair)
+        add_planes(outer, low_pair, exner, exner_pair, ground=True)
 
         @pl.when(is_low)
         def _():
             start(msg["below"])
-            start(msg["below_edge"])
-
-        @pl.when(is_even)
-        def _():
-            start(msg["exner_edge"])
-
-        low_sends += msg["below"] + msg["below_edge"]
+
+        to_rows(msg["below_edge"], is_low)
+        to_rows(msg["exner_edge"], is_even)
+
+        low_sends += msg["below_edge"]
         even_sends += msg["exner_edge"]
+        to_rows(msg["one_up"] + msg["two_up"])
 
         if outer == 0:
-            arrive(msg["plane"])
+
+            @pl.when(early)
+            def _():
+                pl.semaphore_wait(barrier, 4)
+                for condition, copies in held_back:
+                    if condition is None:
+                        start(copies)
+                    else:
+                        pl.when(condition)(functools.partial(start, copies))
+
+            arrive(msg["metric"])
+
+            @pl.when(is_low)
+            def _():
+                arrive(msg["ground"])
+
             coefficients(outer_rows)
         arrive(msg["mass"])
 
@@ -441,22 +517,32 @@
 
         weigh(outer, outer_rows, False)
 
+        @pl.when(is_low)
+        def _():
+            sent(msg["below"])
+
+        @pl.when(is_high)
+        def _():
+            arrive(msg["below"])
+
+        start(msg["one_dn"] + msg["two_dn"])
+        arrive(msg["wind"])
+        run(outer, 0, DYNAMICS)
+
         @pl.when(is_even)
         def _():
             arrive(msg["exner_edge"])
 
         @pl.when(is_high)
         def _():
-            arrive(msg["below"])
             arrive(msg["below_edge"])
 
         montgomery(outer)
-        arrive(msg["wind"])
-        for number in range(3):
+        for number in (1, 2):
             run(outer, number, DYNAMICS)
         previous = msg
 
-    arrive(previous["trace"])
+    arrive(previous["one"] + previous["two"])
     for number in range(3):
         run(OUTER - 1, number, TRACERS)
 
@@ -508,7 +594,7 @@
     plane = VMEM((OUTER, blocks, DEPTH, LANES), jnp.float32)
     volume = VMEM((layers, blocks, DEPTH, LANES), jnp.float32)
     results = pl.pallas_call(
-        functools.partial(steps_kernel, levels, columns, row_devices),
+        functools.partial(steps_kernel, levels, columns, row_devices, PERIOD),
         name="layer_steps",
         out_shape=[part] * 5,
         in_specs=[anywhere] * 5 + [pl.BlockSpec(memory_space=pltpu.SMEM)] + [anywhere] * 3,

time: 60 us -> 52.3 us (0.87)
  Pallas kernels: 59.3 us -> 51.6 us
    pallas_call x1, Pallas kernels: 58.1 us -> 50.4 us  [local(): pl.pallas_call(functools.partial(steps_kernel, levels, columns, row_devic...]
where the time goes in v2:
time: 52.3 us; the launch traced here: 52.2 us
  Pallas kernels  51.6 us (99%)
  between operations  0.64 us (1%)
    pallas_call x1, Pallas kernels, local(): pl.pallas_call(functools.partial(steps_kernel, levels, columns, row_devic...  50.4 us
    pallas_call x1, Pallas kernels, local(): pl.pallas_call(store_kernel, name='store_layers', out_shape=[jax.ShapeDty...  1.13 us

profile of v2, /device:TPU:1, one launch (start us, length us, event | category | flops | bytes accessed | tf_op | source)
XLA Modules:
  0.0 52.2 jit_solution(9242707865120675253)
XLA Ops:
  0.6 50.4 %layer_steps.1 = (f32[4,8,16,128]{3,2,1,0:T(8,128)S(1)}, f32[4,8,16,128]{3,2,1,0:T(8,128)S(1)}, f32[4,8,16,128]{3,2,1,0:T(8,128)S(1)}, f32[4,8,16,128]{3,2,1,0:T(8,128)S(1)}, f32[4,8,16,128]{3,2,1,0:T(8,128)S(1)}) custom-call(f32[4,2,8,8,128]{4,3,2,1,0:T(8,128)} %bitcast.39, f32[4,2,8,8,128]{4,3,2,1,0:T(8,128)} %bitcast.40, f32[4,2,8,8,128]{4,3,2,1,0:T(8,128)} %bitcast.41, ...), custom_call_target="tpu_custom_call" | custom-call | tf_op jit(solution)/shard_map/layer_steps/pallas_call | solution.py:596
  51.1 1.1 %store_layers.1 = (f32[4,2,8,8,128]{4,3,2,1,0:T(8,128)}, f32[4,2,8,8,128]{4,3,2,1,0:T(8,128)}, f32[4,2,8,8,128]{4,3,2,1,0:T(8,128)}, f32[4,2,8,8,128]{4,3,2,1,0:T(8,128)}, f32[4,2,8,8,128]{4,3,2,1,0:T(8,128)}) custom-call(f32[4,8,16,128]{3,2,1,0:T(8,128)S(1)} %get-tuple-element.15.refs_0_, f32[4,8,16,128]{3,2,1,0:T(8,128)S(1)} %get-tuple-element.16.refs_1_, ...), custom_call_target="tpu_custom_call" | custom-call | tf_op jit(solution)/shard_map/store_layers/pallas_call | solution.py:622

commit v3 on v2

--- a/solution.py
+++ b/solution.py
@@ -24,10 +24,11 @@
 LANES = 128
 SUB = 8
 
-TOTAL, PAIR, PAIR_UP, PAIR_DN, TOTAL_UP, TOTAL_DN = range(6)
-EXNER, BELOW, BELOW_UP, BELOW_DN, EXNER_UP, EXNER_DN = range(6, 12)
-MASS_UP, MASS_DN, WIND_UP, WIND_DN, ONE_UP, ONE_DN, TWO_UP, TWO_DN, METRIC_UP, METRIC_DN, GROUND_UP, GROUND_DN = range(12, 24)
-MESSAGES = 24
+SHARE, SHARE_LOW, SHARE_HIGH, TOTAL, TOTAL_UP, TOTAL_DN = range(6)
+EXNER, EXNER_UP, EXNER_DN, GIVE, GIVE_LOW, GIVE_HIGH, BELOW, CROSS_UP, CROSS_DN = range(6, 15)
+MASS_UP, MASS_DN, WIND_UP, WIND_DN, ONE_UP, ONE_DN, TWO_UP, TWO_DN = range(15, 23)
+METRIC_UP, METRIC_DN, GROUND_UP, GROUND_DN = range(23, 27)
+MESSAGES = 27
 
 
 def column_gap(a, edge=False):
@@ -65,13 +66,11 @@
     planes,
     active_raw,
     total,
-    total_pair,
-    pair,
     above,
     exner,
-    exner_pair,
-    low_pair,
     below,
+    shared,
+    given,
     weight,
     potential,
     slope_x,
@@ -93,7 +92,12 @@
     far_lev = lax.rem(lev + 2, 4)
     far, far_up, far_dn = (far_lev, row), (far_lev, up_row), (far_lev, dn_row)
     up, dn = (lev, up_row), (lev, dn_row)
-    is_odd, is_even = odd == 1, odd == 0
+    cross_lev = far_lev + 1 - 2 * odd
+    cross_up, cross_dn = (cross_lev, up_row), (cross_lev, dn_row)
+    is_even = odd == 0
+    half_blocks = blocks // 2
+    mine = pl.ds(odd * half_blocks, half_blocks)
+    theirs = pl.ds((1 - odd) * half_blocks, half_blocks)
     is_high, is_low = lev < 2, lev >= 2
     own = pl.ds(OWN, 2 * SUB)
     first_layer = lev * layers
@@ -133,29 +137,29 @@
 
     @pl.when(late & jnp.logical_not(up_early))
     def _():
-        greet(up, far_up)
+        greet(up, far_up, cross_up)
 
     @pl.when(late & jnp.logical_not(dn_early))
     def _():
-        greet(dn, far_dn)
+        greet(dn, far_dn, cross_dn)
 
     def meet():
         @pl.when(early)
         def _():
             pl.semaphore_wait(barrier, 2)
-            greet(up, far_up, dn, far_dn)
+            greet(up, far_up, cross_up, dn, far_dn, cross_dn)
 
         @pl.when(late)
         def _():
-            pl.semaphore_wait(barrier, 6)
+            pl.semaphore_wait(barrier, 8)
 
         @pl.when(late & up_early)
         def _():
-            greet(up, far_up)
+            greet(up, far_up, cross_up)
 
         @pl.when(late & dn_early)
         def _():
-            greet(dn, far_dn)
+            greet(dn, far_dn, cross_dn)
 
     def message(outer, kind, source, target, device):
         return pltpu.make_async_remote_copy(
@@ -185,22 +189,43 @@
     def all_messages(outer):
         same = lambda kinds, ref: edges(outer, kinds, ref, ref, up, dn)
         msg = {}
-        msg["total"] = [message(outer, TOTAL, total.at[outer, :, own, :], total_pair.at[outer, :, own, :], core)]
-        msg["pair"] = [
-            message(outer, PAIR, pair.at[outer, :, own, :], above.at[outer, :, own, :], far)
-        ]
-        msg["pair_edge"] = edges(
-            outer, (PAIR_UP, PAIR_DN), plane_rows(pair, outer), plane_rows(above, outer), far_up, far_dn
+        low_rows, high_rows = edge_up[1], edge_dn[1]
+
+        def to_core(kinds, ref, ref_to):
+            return [
+                message(outer, kind, ref(rows), ref_to(rows), core)
+                for kind, rows in zip(kinds, (own, low_rows, high_rows))
+            ]
+
+        half_below = lambda rows: below.at[outer, mine, rows, :]
+        for name, copies in (
+            (
+                "share",
+                to_core(
+                    (SHARE, SHARE_LOW, SHARE_HIGH),
+                    lambda rows: state.at[outer, 2, :, theirs, rows, :],
+                    lambda rows: shared.at[outer, :, :, rows, :],
+                ),
+            ),
+            (
+                "give",
+                to_core(
+                    (GIVE, GIVE_LOW, GIVE_HIGH),
+                    lambda rows: given.at[outer, :, :, rows, :],
+                    lambda rows: weight.at[outer, :, mine, rows, :],
+                ),
+            ),
+        ):
+            msg[name], msg[name + "_edge"] = copies[:1], copies[1:]
+        msg["total"] = [message(outer, TOTAL, total.at[outer, :, own, :], above.at[outer, :, own, :], far)]
+        msg["total_edge"] = edges(
+            outer, (TOTAL_UP, TOTAL_DN), plane_rows(total, outer), plane_rows(above, outer), far_up, far_dn
         )
-        msg["total_edge"] = same((TOTAL_UP, TOTAL_DN), plane_rows(total_pair, outer))
-        msg["exner"] = [message(outer, EXNER, exner.at[outer, :, own, :], exner_pair.at[outer, :, own, :], core)]
-        msg["below"] = [
-            message(outer, BELOW, low_pair.at[outer, :, own, :], below.at[outer, :, own, :], far)
-        ]
-        msg["below_edge"] = edges(
-            outer, (BELOW_UP, BELOW_DN), plane_rows(low_pair, outer), plane_rows(below, outer), far_up, far_dn
-        )
-        msg["exner_edge"] = same((EXNER_UP, EXNER_DN), plane_rows(exner_pair, outer))
+        msg["exner"] = [message(outer, EXNER, exner.at[outer, :, own, :], half_below(own), far)]
+        msg["below"] = [message(outer, BELOW, half_below(own), half_below(own), core)]
+        msg["exner_edge"] = edges(
+            outer, (EXNER_UP, EXNER_DN), plane_rows(exner, outer), half_below, far_up, far_dn
+        ) + edges(outer, (CROSS_UP, CROSS_DN), plane_rows(exner, outer), half_below, cross_up, cross_dn)
         for name, kinds, ref in (
             ("mass", (MASS_UP, MASS_DN), field_rows(outer, 2, 1)),
             ("wind", (WIND_UP, WIND_DN), field_rows(outer, 0, 2)),
@@ -236,41 +261,37 @@
     def sum_layers(outer):
         def body(tile):
             rows = pl.ds(OWN + SUB * tile, SUB)
-            acc = jnp.abs(state[outer, 2, 0, :, rows, :])
+            acc = jnp.abs(state[outer, 2, 0, mine, rows, :]) + jnp.abs(shared[outer, 0, :, rows, :])
             for layer in range(1, layers):
-                acc = acc + jnp.abs(state[outer, 2, layer, :, rows, :])
+                acc = acc + (jnp.abs(state[outer, 2, layer, mine, rows, :]) + jnp.abs(shared[outer, layer, :, rows, :]))
             total[outer, :, rows, :] = acc
-
-        tiles(2, body, 2)
-
-    def add_planes(outer, out, one, other, ground=False):
-        def body(tile):
-            rows = pl.ds(OWN + SUB * tile, SUB)
-            both = one[outer, :, rows, :] + other[outer, :, rows, :]
-            out[outer, :, rows, :] = both + planes[1, :, rows, :] if ground else both
 
         tiles(2, body, 2)
 
     def weigh(outer, starts, keep_sum):
         base, stride = starts
+        chip_layer = first_layer - odd * layers
 
         def body(tile):
             rows = pl.ds(base + stride * tile, SUB)
-            running = jnp.where(is_odd, total_pair[outer, :, rows, :], 0.0) + jnp.where(
-                is_low, above[outer, :, rows, :], 0.0
-            )
-            weighted = []
+            running = jnp.where(is_low, above[outer, :, rows, :], 0.0)
+            ours = [state[outer, 2, layer, mine, rows, :] for layer in range(layers)]
+            others = [shared[outer, layer, :, rows, :] for layer in range(layers)]
+            column = [jnp.where(is_even, a, b) for a, b in zip(ours, others)]
+            column += [jnp.where(is_even, b, a) for a, b in zip(ours, others)]
+            sums = []
+            for layer, mass in enumerate(column):
+                running = running + jnp.abs(mass)
+                pressure = top_pressure + running * (1.0 / levels)
+                sums.append(theta[chip_layer + layer] * jnp.exp(exner_power * jnp.log(pressure)))
+            for layer in range(2 * layers - 2, -1, -1):
+                sums[layer] = sums[layer] + sums[layer + 1]
             for layer in range(layers):
-                running = running + jnp.abs(state[outer, 2, layer, :, rows, :])
-                pressure = top_pressure + running * (1.0 / levels)
-                weighted.append(theta[first_layer + layer] * jnp.exp(exner_power * jnp.log(pressure)))
-            acc = weighted[-1]
-            weight[layers - 1, :, rows, :] = acc
-            for layer in range(layers - 2, -1, -1):
-                acc = acc + weighted[layer]
-                weight[layer, :, rows, :] = acc
+                upper, lower = sums[layer], sums[layer + layers]
+                weight[outer, layer, mine, rows, :] = jnp.where(is_even, upper, lower)
+                given[outer, layer, :, rows, :] = jnp.where(is_even, lower, upper)
             if keep_sum:
-                exner[outer, :, rows, :] = acc
+                exner[outer, :, rows, :] = sums[0] + planes[1, mine, rows, :]
 
         tiles(2, body)
 
@@ -295,19 +316,20 @@
 
         tiles(2, body)
 
-    def montgomery(outer):
+    def montgomery(outer, starts):
+        base, stride = starts
+
         def body(tile):
-            rows = pl.ds(OWN - 4 + SUB * tile, SUB)
-            rest = jnp.where(is_even, exner_pair[outer, :, rows, :], 0.0) + jnp.where(
-                is_high, below[outer, :, rows, :], planes[1, :, rows, :]
-            )
+            rows = pl.ds(base + stride * tile, SUB)
+            rest = jnp.where(is_high, below[outer, :, rows, :], planes[1, :, rows, :])
             for layer in range(layers):
-                potential[layer, :, rows, :] = rest + weight[layer, :, rows, :]
-
-        tiles(3, body, 3)
-
-        def slopes(index):
-            layer, tile = index // 3, lax.rem(index, 3)
+                potential[layer, :, rows, :] = rest + weight[outer, layer, :, rows, :]
+
+        tiles(2, body, 2)
+
+    def slopes(picked):
+        def body(index):
+            layer, tile = pick(picked, index)
             base = OWN - 4 + SUB * tile
             rows = pl.ds(base, SUB)
             half = half_metric[layer, :, rows, :]
@@ -320,16 +342,20 @@
             first[0, layer, :, rows, :] = first[0, layer, :, rows, :] - (time_step * SECTIONS[0]) * along
             first[1, layer, :, rows, :] = first[1, layer, :, rows, :] - (time_step * SECTIONS[0]) * across
 
-        tiles(3 * layers, slopes, 4)
-
-    def section(outer, number, fields, results):
-        count = 2 if number == 2 else 3
+        tiles(picked[0] * layers, body, 4)
+
+    def pick(picked, index):
+        count, begin, stride = picked
+        return index // count, begin + stride * lax.rem(index, count)
+
+    def section(outer, number, fields, results, picked=None):
+        picked = picked or (2 if number == 2 else 3, 0, 1)
         begin = OWN if number == 2 else OWN - 4
         factor = time_step * SECTIONS[number]
         source = (state.at[outer], first, second)[number]
 
         def body(index):
-            layer, tile = index // count, lax.rem(index, count)
+            layer, tile = pick(picked, index)
             base = begin + SUB * tile
 
             def get(ref, field, shift=0):
@@ -367,7 +393,7 @@
                 if field > 2:
                     results(field, layer, tile)[...] = get(start_of, field) - carried(field)
 
-        tiles(count * layers, body, 4)
+        tiles(picked[0] * layers, body, 4)
 
     def plane_of(ref, base):
         return ref[:, pl.ds(base, SUB), :]
@@ -384,14 +410,14 @@
 
     DYNAMICS, TRACERS = (0, 1, 2), (3, 4)
 
-    def run(outer, number, fields):
-        section(outer, number, fields, results_of(outer, number))
+    def run(outer, number, fields, picked=None):
+        section(outer, number, fields, results_of(outer, number), picked)
+
+    middle, beside = (1, 1, 0), (2, 0, 2)
 
     inner = (OWN, SUB)
     outer_rows = (OWN - SUB, 3 * SUB)
-    sends = []
-    high_sends, low_sends, odd_sends, even_sends = [], [], [], []
-
+    sends, high_sends, low_sends = [], [], []
     previous = None
     held_back = []
     for outer in range(OUTER):
@@ -407,12 +433,16 @@
             else:
                 pl.when(allowed)(functools.partial(start, copies))
 
+        sends += msg["share"] + msg["share_edge"] + msg["give"] + msg["give_edge"]
+        sends += msg["mass"] + msg["wind"] + msg["one"] + msg["two"]
+        high_sends += msg["total_edge"] + msg["below"]
+        low_sends += msg["exner_edge"]
+
         if outer == 0:
             for copy in loads_mass:
                 copy.wait()
-            sum_layers(outer)
             meet()
-            start(msg["total"])
+            start(msg["share"])
             to_rows(msg["mass"])
             for copy in loads_planes:
                 copy.wait()
@@ -429,69 +459,56 @@
             for copy in loads_wind:
                 copy.wait()
         else:
+            start(msg["share"])
+            to_rows(msg["mass"])
+
+        arrive(msg["share"])
+
+        @pl.when(is_high)
+        def _():
             sum_layers(outer)
             start(msg["total"])
-            to_rows(msg["mass"])
-            arrive(previous["one"] + previous["two"])
-            run(outer - 1, 0, TRACERS)
-        sends += msg["total"] + msg["mass"] + msg["wind"] + msg["exner"] + msg["one"] + msg["two"]
-
-        arrive(msg["total"])
-        add_planes(outer, pair, total, total_pair)
-
-        @pl.when(is_high)
-        def _():
-            start(msg["pair"])
-
-        to_rows(msg["pair_edge"], is_high)
-        to_rows(msg["total_edge"], is_odd)
-
-        high_sends += msg["pair_edge"]
-        odd_sends += msg["total_edge"]
+
+        to_rows(msg["total_edge"], is_high)
         to_rows(msg["wind_dn"])
 
         if outer == 0:
             coefficients(inner)
             for copy in loads_trace:
                 copy.wait()
-        else:
-            run(outer - 1, 1, TRACERS)
+
+        @pl.when(is_low)
+        def _():
+            arrive(msg["total"])
+
+        weigh(outer, inner, True)
+        start(msg["give"])
+
+        @pl.when(is_low)
+        def _():
+            start(msg["exner"])
+
+        to_rows(msg["exner_edge"], is_low)
 
         @pl.when(is_high)
         def _():
-            sent(msg["pair"])
-
-        @pl.when(is_low)
-        def _():
-            arrive(msg["pair"])
+            sent(msg["total"])
 
         if outer == 0:
             to_rows(msg["metric_up"])
             to_rows(msg["ground_up"], is_low)
         to_rows(msg["wind_up"])
-        weigh(outer, inner, True)
-        start(msg["exner"])
         if outer > 0:
-            run(outer - 1, 2, TRACERS)
-        arrive(msg["exner"])
-        add_planes(outer, low_pair, exner, exner_pair, ground=True)
-
-        @pl.when(is_low)
-        def _():
-            start(msg["below"])
-
-        to_rows(msg["below_edge"], is_low)
-        to_rows(msg["exner_edge"], is_even)
-
-        low_sends += msg["below_edge"]
-        even_sends += msg["exner_edge"]
+            arrive(previous["one"] + previous["two"])
+            for number in range(3):
+                run(outer - 1, number, TRACERS)
         to_rows(msg["one_up"] + msg["two_up"])
 
         if outer == 0:
 
             @pl.when(early)
             def _():
-                pl.semaphore_wait(barrier, 4)
+                pl.semaphore_wait(barrier, 6)
                 for condition, copies in held_back:
                     if condition is None:
                         start(copies)
@@ -506,38 +523,46 @@
 
             coefficients(outer_rows)
         arrive(msg["mass"])
-
-        @pl.when(is_odd)
+        start(msg["share_edge"])
+
+        @pl.when(is_low)
+        def _():
+            sent(msg["exner"])
+
+        @pl.when(is_high)
+        def _():
+            arrive(msg["exner"])
+            start(msg["below"])
+
+        start(msg["one_dn"] + msg["two_dn"])
+        arrive(msg["share_edge"])
+
+        @pl.when(is_low)
         def _():
             arrive(msg["total_edge"])
 
-        @pl.when(is_low)
-        def _():
-            arrive(msg["pair_edge"])
-
         weigh(outer, outer_rows, False)
-
-        @pl.when(is_low)
-        def _():
-            sent(msg["below"])
+        start(msg["give_edge"])
+
+        run(outer, 0, DYNAMICS, middle)
+        arrive(msg["give"])
 
         @pl.when(is_high)
         def _():
             arrive(msg["below"])
 
-        start(msg["one_dn"] + msg["two_dn"])
+        montgomery(outer, inner)
+        slopes(middle)
         arrive(msg["wind"])
-        run(outer, 0, DYNAMICS)
-
-        @pl.when(is_even)
+        run(outer, 0, DYNAMICS, beside)
+        arrive(msg["give_edge"])
+
+        @pl.when(is_high)
         def _():
             arrive(msg["exner_edge"])
 
-        @pl.when(is_high)
-        def _():
-            arrive(msg["below_edge"])
-
-        montgomery(outer)
+        montgomery(outer, outer_rows)
+        slopes(beside)
         for number in (1, 2):
             run(outer, number, DYNAMICS)
         previous = msg
@@ -550,8 +575,6 @@
     for condition, copies in (
         (is_high, high_sends),
         (is_low, low_sends),
-        (is_odd, odd_sends),
-        (is_even, even_sends),
     ):
 
         @pl.when(condition)
@@ -591,7 +614,7 @@
     anywhere = pl.BlockSpec(memory_space=pltpu.HBM)
     in_vmem = pl.BlockSpec(memory_space=VMEM)
     part = jax.ShapeDtypeStruct((layers, blocks, rows, LANES), jnp.float32)
-    plane = VMEM((OUTER, blocks, DEPTH, LANES), jnp.float32)
+    half_plane = VMEM((OUTER, blocks // 2, DEPTH, LANES), jnp.float32)
     volume = VMEM((layers, blocks, DEPTH, LANES), jnp.float32)
     results = pl.pallas_call(
         functools.partial(steps_kernel, levels, columns, row_devices, PERIOD),
@@ -606,8 +629,11 @@
             VMEM((3, blocks, DEPTH, LANES), jnp.float32),
             VMEM((blocks, DEPTH, LANES), jnp.int32),
         ]
-        + [plane] * 8
-        + [volume] * 7
+        + [half_plane] * 3
+        + [VMEM((OUTER, blocks, DEPTH, LANES), jnp.float32)]
+        + [VMEM((OUTER, layers, blocks // 2, DEPTH, LANES), jnp.float32)] * 2
+        + [VMEM((OUTER, layers, blocks, DEPTH, LANES), jnp.float32)]
+        + [volume] * 6
         + [
             VMEM((blocks, DEPTH, LANES), jnp.float32),
             pltpu.SemaphoreType.DMA((8, 2)),

time: 52.3 us -> 50.5 us (0.966)
  Pallas kernels: 51.6 us -> 49.7 us
    pallas_call x1, Pallas kernels: 50.4 us -> 48.6 us  [local(): pl.pallas_call(functools.partial(steps_kernel, levels, columns, row_devic...]
where the time goes in v3:
time: 50.5 us; the launch traced here: 50.4 us
  Pallas kernels  49.7 us (98%)
  between operations  0.64 us (1%)
    pallas_call x1, Pallas kernels, local(): pl.pallas_call(functools.partial(steps_kernel, levels, columns, row_devic...  48.6 us
    pallas_call x1, Pallas kernels, local(): pl.pallas_call(store_kernel, name='store_layers', out_shape=[jax.ShapeDty...  1.13 us

profile of v3, /device:TPU:1, one launch (start us, length us, event | category | flops | bytes accessed | tf_op | source)
XLA Modules:
  0.0 50.4 jit_solution(13530086581368613749)
XLA Ops:
  0.6 48.6 %layer_steps.1 = (f32[4,8,16,128]{3,2,1,0:T(8,128)S(1)}, f32[4,8,16,128]{3,2,1,0:T(8,128)S(1)}, f32[4,8,16,128]{3,2,1,0:T(8,128)S(1)}, f32[4,8,16,128]{3,2,1,0:T(8,128)S(1)}, f32[4,8,16,128]{3,2,1,0:T(8,128)S(1)}) custom-call(f32[4,2,8,8,128]{4,3,2,1,0:T(8,128)} %bitcast.39, f32[4,2,8,8,128]{4,3,2,1,0:T(8,128)} %bitcast.40, f32[4,2,8,8,128]{4,3,2,1,0:T(8,128)} %bitcast.41, ...), custom_call_target="tpu_custom_call" | custom-call | tf_op jit(solution)/shard_map/layer_steps/pallas_call | solution.py:619
  49.2 1.1 %store_layers.1 = (f32[4,2,8,8,128]{4,3,2,1,0:T(8,128)}, f32[4,2,8,8,128]{4,3,2,1,0:T(8,128)}, f32[4,2,8,8,128]{4,3,2,1,0:T(8,128)}, f32[4,2,8,8,128]{4,3,2,1,0:T(8,128)}, f32[4,2,8,8,128]{4,3,2,1,0:T(8,128)}) custom-call(f32[4,8,16,128]{3,2,1,0:T(8,128)S(1)} %get-tuple-element.15.refs_0_, f32[4,8,16,128]{3,2,1,0:T(8,128)S(1)} %get-tuple-element.16.refs_1_, ...), custom_call_target="tpu_custom_call" | custom-call | tf_op jit(solution)/shard_map/store_layers/pallas_call | solution.py:648

commit v4 on v3

--- a/solution.py
+++ b/solution.py
@@ -342,7 +342,7 @@
             first[0, layer, :, rows, :] = first[0, layer, :, rows, :] - (time_step * SECTIONS[0]) * along
             first[1, layer, :, rows, :] = first[1, layer, :, rows, :] - (time_step * SECTIONS[0]) * across
 
-        tiles(picked[0] * layers, body, 4)
+        tiles(picked[0] * layers, body, 4 if picked[0] != 2 else 8)
 
     def pick(picked, index):
         count, begin, stride = picked
@@ -393,7 +393,7 @@
                 if field > 2:
                     results(field, layer, tile)[...] = get(start_of, field) - carried(field)
 
-        tiles(picked[0] * layers, body, 4)
+        tiles(picked[0] * layers, body, 4 if picked[0] != 2 else 8)
 
     def plane_of(ref, base):
         return ref[:, pl.ds(base, SUB), :]
@@ -567,8 +567,10 @@
             run(outer, number, DYNAMICS)
         previous = msg
 
+    run(OUTER - 1, 0, TRACERS, middle)
     arrive(previous["one"] + previous["two"])
-    for number in range(3):
+    run(OUTER - 1, 0, TRACERS, beside)
+    for number in (1, 2):
         run(OUTER - 1, number, TRACERS)
 
     sent(sends)

time: 50.5 us -> 49.9 us (0.988)
    pallas_call x1, Pallas kernels: 48.6 us -> 48 us  [local(): pl.pallas_call(functools.partial(steps_kernel, levels, columns, row_devic...]
where the time goes in v4:
time: 49.9 us; the launch traced here: 49.8 us
  Pallas kernels  49.2 us (99%)
  between operations  0.64 us (1%)
    pallas_call x1, Pallas kernels, local(): pl.pallas_call(functools.partial(steps_kernel, levels, columns, row_devic...  48 us
    pallas_call x1, Pallas kernels, local(): pl.pallas_call(store_kernel, name='store_layers', out_shape=[jax.ShapeDty...  1.13 us

profile of v4, /device:TPU:1, one launch (start us, length us, event | category | flops | bytes accessed | tf_op | source)
XLA Modules:
  0.0 49.8 jit_solution(379742238083530849)
XLA Ops:
  0.6 48.0 %layer_steps.1 = (f32[4,8,16,128]{3,2,1,0:T(8,128)S(1)}, f32[4,8,16,128]{3,2,1,0:T(8,128)S(1)}, f32[4,8,16,128]{3,2,1,0:T(8,128)S(1)}, f32[4,8,16,128]{3,2,1,0:T(8,128)S(1)}, f32[4,8,16,128]{3,2,1,0:T(8,128)S(1)}) custom-call(f32[4,2,8,8,128]{4,3,2,1,0:T(8,128)} %bitcast.39, f32[4,2,8,8,128]{4,3,2,1,0:T(8,128)} %bitcast.40, f32[4,2,8,8,128]{4,3,2,1,0:T(8,128)} %bitcast.41, ...), custom_call_target="tpu_custom_call" | custom-call | tf_op jit(solution)/shard_map/layer_steps/pallas_call | solution.py:621
  48.7 1.1 %store_layers.1 = (f32[4,2,8,8,128]{4,3,2,1,0:T(8,128)}, f32[4,2,8,8,128]{4,3,2,1,0:T(8,128)}, f32[4,2,8,8,128]{4,3,2,1,0:T(8,128)}, f32[4,2,8,8,128]{4,3,2,1,0:T(8,128)}, f32[4,2,8,8,128]{4,3,2,1,0:T(8,128)}) custom-call(f32[4,8,16,128]{3,2,1,0:T(8,128)S(1)} %get-tuple-element.15.refs_0_, f32[4,8,16,128]{3,2,1,0:T(8,128)S(1)} %get-tuple-element.16.refs_1_, ...), custom_call_target="tpu_custom_call" | custom-call | tf_op jit(solution)/shard_map/store_layers/pallas_call | solution.py:650

commit v5 on v4

--- a/solution.py
+++ b/solution.py
@@ -293,7 +293,7 @@
             if keep_sum:
                 exner[outer, :, rows, :] = sums[0] + planes[1, mine, rows, :]
 
-        tiles(2, body)
+        tiles(2, body, 2)
 
     def coefficients(starts):
         base, stride = starts
@@ -482,13 +482,13 @@
             arrive(msg["total"])
 
         weigh(outer, inner, True)
+
+        @pl.when(is_low)
+        def _():
+            start(msg["exner"])
+
+        to_rows(msg["exner_edge"], is_low)
         start(msg["give"])
-
-        @pl.when(is_low)
-        def _():
-            start(msg["exner"])
-
-        to_rows(msg["exner_edge"], is_low)
 
         @pl.when(is_high)
         def _():

time: 49.9 us -> 49.9 us (level)
  no operation moved by 1% of the time
where the time goes in v5:
time: 49.9 us; the launch traced here: 49.8 us
  Pallas kernels  49.2 us (99%)
  between operations  0.64 us (1%)
    pallas_call x1, Pallas kernels, local(): pl.pallas_call(functools.partial(steps_kernel, levels, columns, row_devic...  48 us
    pallas_call x1, Pallas kernels, local(): pl.pallas_call(store_kernel, name='store_layers', out_shape=[jax.ShapeDty...  1.13 us

profile of v5, /device:TPU:1, one launch (start us, length us, event | category | flops | bytes accessed | tf_op | source)
XLA Modules:
  0.0 49.8 jit_solution(5350468766866117019)
XLA Ops:
  0.6 48.0 %layer_steps.1 = (f32[4,8,16,128]{3,2,1,0:T(8,128)S(1)}, f32[4,8,16,128]{3,2,1,0:T(8,128)S(1)}, f32[4,8,16,128]{3,2,1,0:T(8,128)S(1)}, f32[4,8,16,128]{3,2,1,0:T(8,128)S(1)}, f32[4,8,16,128]{3,2,1,0:T(8,128)S(1)}) custom-call(f32[4,2,8,8,128]{4,3,2,1,0:T(8,128)} %bitcast.39, f32[4,2,8,8,128]{4,3,2,1,0:T(8,128)} %bitcast.40, f32[4,2,8,8,128]{4,3,2,1,0:T(8,128)} %bitcast.41, ...), custom_call_target="tpu_custom_call" | custom-call | tf_op jit(solution)/shard_map/layer_steps/pallas_call | solution.py:621
  48.7 1.1 %store_layers.1 = (f32[4,2,8,8,128]{4,3,2,1,0:T(8,128)}, f32[4,2,8,8,128]{4,3,2,1,0:T(8,128)}, f32[4,2,8,8,128]{4,3,2,1,0:T(8,128)}, f32[4,2,8,8,128]{4,3,2,1,0:T(8,128)}, f32[4,2,8,8,128]{4,3,2,1,0:T(8,128)}) custom-call(f32[4,8,16,128]{3,2,1,0:T(8,128)S(1)} %get-tuple-element.15.refs_0_, f32[4,8,16,128]{3,2,1,0:T(8,128)S(1)} %get-tuple-element.16.refs_1_, ...), custom_call_target="tpu_custom_call" | custom-call | tf_op jit(solution)/shard_map/store_layers/pallas_call | solution.py:650
